TPU v7x, 32 devices: a whole 2x2x4 slice. The times are simulated.
32 devices in a mesh: replica: 2 (over y), tensor: 2 (over x), group: 8 (over z, core).
Axes of the slice: x: 2, y: 2, z: 4, core: 2. Of those that a mesh axis runs over, the one named last changes fastest.
Arguments:
- hidden_in: bfloat16 [16, 512, 5120], P(('replica', 'group'), None, 'tensor'), parts along dimension 0, may hold values from -6 to 6
- ln_gain: bfloat16 [5120], P('tensor'), may hold values from 0.25 to 1.75
- wq: bfloat16 [5120, 4096], P(None, 'tensor'), may hold values from -0.078125 to 0.078125
- wk: bfloat16 [5120, 1024], P(None, 'tensor'), may hold values from -0.078125 to 0.078125
- wv: bfloat16 [5120, 1024], P(None, 'tensor'), may hold values from -0.078125 to 0.078125
- q_gain: bfloat16 [128], replicated, may hold values from 0.7 to 6
- key_norm_gain: bfloat16 [128], replicated, may hold values from 0.7 to 6
- wo: bfloat16 [4096, 5120], P('tensor'), may hold values from -0.5 to 0.5
- prompt_spans: int32 [6], P('replica'), parts along dimension 0, may hold values from 1 to 4, 8 in all
- span_source: int32 [16], P('replica'), parts along dimension 0, may hold values from 0 to 7, each once
- span_target: int32 [16], P('replica'), parts along dimension 0, may hold values from 0 to 7, each once
- page_slot: int32 [64], P('replica'), parts along dimension 0, may hold values from 0 to 31, each once
Outputs:
- mixed: bfloat16 [16, 512, 5120], P(('replica', 'group'), None, 'tensor'), parts along dimension 0
- kv_pages: bfloat16 [64, 2, 128, 1024], P(('replica', 'group')), parts along dimension 0
There are 2 independent parts, one for each index of `replica`. A program takes and returns all parts, laid end to end along the dimension named above; an argument that names none is the same for every part. Nothing has to cross between parts.
Inputs may be any that keep to these rules, and one draw needn't show every extreme that they name: `prompt_spans`: the lengths sum to 8; the longest prompt has exactly 4 spans. `span_source`: a permutation of the slots. `span_target`: a permutation of the slots. `page_slot`: a permutation of the page slots.
All inputs are finite; a program needn't handle non-finite values.
Results may differ from a plain program's by a relative error of at most 0.011.
The roundings to bfloat16 on the way count: a program that leaves them out, or rounds other values in their place, can miss the bound.
Values may be sent and summed in bfloat16 or wider, within the bound.
No kernel may reach another device: no remote copies, remote signals or barrier semaphores. Data moves between devices by JAX's collectives and lax.ppermute only.
A program may use at most 576 MiB of HBM per device.

v0:
```python
import functools
import math

import jax
import jax.numpy as jnp
from jax import lax
from jax.experimental import pallas as pl
from jax.experimental.pallas import tpu as pltpu
from jax.sharding import PartitionSpec as P

PAGE_ROWS = 128
epsilon = 1e-06
rope_base = 1000000.0
very_negative = -1e30
PARTS = 2
CORES = 2
SHARE = 0.02


def params(mebibytes):
    return pltpu.CompilerParams(vmem_limit_bytes=mebibytes * 1024 * 1024)


def in_hbm(x):
    return pltpu.with_memory_space_constraint(x, pltpu.HBM)


def cost(flops, moved, transcendentals=0):
    return pl.CostEstimate(
        flops=int(flops * SHARE),
        bytes_accessed=int(moved * SHARE),
        transcendentals=int(transcendentals * SHARE),
    )


def hop_order(chips):
    return [0, 1, chips - 1] + list(range(2, chips - 1)) if chips > 2 else list(range(chips))


class Layout:
    def __init__(self, spans, pages, owners):
        self.chips = owners // CORES
        self.span_at = 0
        self.earlier_at = self.span_at + spans
        self.target_at = self.earlier_at + spans
        self.sent_as = self.target_at + spans
        self.page = self.sent_as + spans
        self.origin = self.page + pages
        self.group_rank = self.origin + owners * spans
        self.tensor_rank = self.group_rank + 1
        self.length = self.tensor_rank + 1


def tables_kernel(lay, spans, pages, ranks, prompt_spans, source, target, page_slot, out, span_of, start_of):
    chips = lay.chips
    group_rank = ranks[0]
    out[lay.group_rank] = group_rank
    out[lay.tensor_rank] = ranks[1]
    for k in range(spans):
        start = jnp.int32(0)
        begin = jnp.int32(0)
        for p in range(prompt_spans.shape[0]):
            start = jnp.where(begin <= k, begin, start)
            begin = begin + prompt_spans[p]
        start_of[k] = start
        span_of[source[k]] = jnp.int32(k)
    for p in range(pages):
        out[lay.page + page_slot[p]] = jnp.int32(p)
    chip, core = lax.div(group_rank, CORES), lax.rem(group_rank, CORES)
    hops = hop_order(chips)
    for back in range(chips):
        for other in range(CORES):
            at_chip = lax.rem(chip + chips - back, chips)
            at_core = jnp.where(other == 0, core, 1 - core)
            for n, hop in enumerate(hops):
                for flip in range(CORES):
                    from_chip = lax.rem(at_chip + chips - hop, chips)
                    from_core = jnp.where(flip == 0, at_core, 1 - at_core)
                    k = span_of[from_chip * CORES + from_core]
                    place = n * CORES + flip
                    out[lay.origin + (back * CORES + other) * spans + place] = k
                    if back == 0 and other == 0:
                        out[lay.span_at + place] = k
                        out[lay.earlier_at + place] = k - start_of[k]
                        owner = target[k]
                        ahead = lax.rem(lax.div(owner, CORES) + chips - chip, chips)
                        turn = jnp.int32(0)
                        for m, other_hop in enumerate(hops):
                            turn = jnp.where(ahead == other_hop, jnp.int32(m), turn)
                        crossing = jnp.where(lax.rem(owner, CORES) == core, 0, 1)
                        out[lay.target_at + place] = owner
                        out[lay.sent_as + place] = turn * CORES + crossing


def make_tables(lay, spans, pages, ranks, prompt_spans, source, target, page_slot):
    smem = pl.BlockSpec(memory_space=pltpu.SMEM)
    return pl.pallas_call(
        functools.partial(tables_kernel, lay, spans, pages),
        out_shape=jax.ShapeDtypeStruct((lay.length,), jnp.int32),
        in_specs=[smem] * 5,
        out_specs=smem,
        scratch_shapes=[pltpu.SMEM((spans,), jnp.int32)] * 2,
        compiler_params=params(4),
        name="tables",
    )(ranks, prompt_spans, source, target, page_slot)


def head_norm_rope(u, gain, cosine, sine):
    mean_sq = jnp.mean(u * u, axis=-1, keepdims=True)
    u = u * lax.rsqrt(mean_sq + epsilon) * gain
    half = u.shape[-1] // 2
    return u * cosine + pltpu.roll(u, half, 1) * sine


def half_index(lay, sides, side):
    if sides == 1:
        return lambda t: 0
    if side == 0:
        return lambda t: t[lay.tensor_rank]
    return lambda t: 1 - t[lay.tensor_rank]


def summed_dot(lefts, rights):
    total = None
    for left, right in zip(lefts, rights):
        term = jnp.dot(left[...], right[...], preferred_element_type=jnp.float32)
        total = term if total is None else total + term
    return total


def kv_kernel(sides, blocks, table, *refs):
    refs = list(refs)
    take = lambda n: [refs.pop(0) for _ in range(n)]
    xs = [take(blocks) for _ in range(sides)]
    gains, wks, wvs = take(sides), take(sides), take(sides)
    kgain, cosine, sine = take(3)
    normed, (kv,) = take(sides), take(1)
    head = kgain.shape[1]
    width = sum(x[0].shape[1] for x in xs)

    @pl.when(pl.program_id(0) == 0)
    def _():
        at = 0
        for b in range(blocks):
            wide = [x[b][...].astype(jnp.float32) for x in xs]
            total = sum(jnp.sum(w * w, axis=-1, keepdims=True) for w in wide)
            factor = lax.rsqrt(total / width + epsilon)
            rows = xs[0][b].shape[0]
            for w, gain, to in zip(wide, gains, normed):
                to[at : at + rows] = (w * factor * gain[...].astype(jnp.float32)).astype(
                    jnp.bfloat16
                )
            at += rows

    keys = summed_dot(normed, wks).astype(jnp.bfloat16)
    gains = kgain[...].astype(jnp.float32)
    for h in range(keys.shape[1] // head):
        u = keys[:, h * head : (h + 1) * head].astype(jnp.float32)
        kv[0, :, h * head : (h + 1) * head] = head_norm_rope(
            u, gains, cosine[...], sine[...]
        ).astype(jnp.bfloat16)
    kv[1] = summed_dot(normed, wvs).astype(jnp.bfloat16)


def make_kv(lay, table, xs, gains, wk, wv, kgain, cosine, sine, part):
    sides, blocks = len(xs), len(xs[0])
    rows = sum(x.shape[0] for x in xs[0])
    widths = [x[0].shape[1] for x in xs]
    width, cols = wk.shape
    tile = 256 if cols % 256 == 0 else cols
    head = kgain.shape[1]
    fixed = lambda n, t: (0, 0)
    here = lambda n, t: (part, 0)
    weights = []
    for side in range(sides):
        index = half_index(lay, sides, side)
        weights.append(
            pl.BlockSpec((widths[side], tile), lambda n, t, index=index: (index(t), n))
        )
    return pl.pallas_call(
        functools.partial(kv_kernel, sides, blocks),
        grid_spec=pltpu.PrefetchScalarGridSpec(
            num_scalar_prefetch=1,
            grid=(cols // tile,),
            in_specs=[pl.BlockSpec(x.shape, fixed) for side in xs for x in side]
            + [pl.BlockSpec((1, w), fixed) for w in widths]
            + weights
            + weights
            + [
                pl.BlockSpec((1, head), fixed),
                pl.BlockSpec((rows, head), here),
                pl.BlockSpec((rows, head), here),
            ],
            out_specs=[pl.BlockSpec((rows, w), fixed) for w in widths]
            + [pl.BlockSpec((2, rows, tile), lambda n, t: (0, 0, n))],
        ),
        out_shape=[jax.ShapeDtypeStruct((rows, w), jnp.bfloat16) for w in widths]
        + [jax.ShapeDtypeStruct((2, rows, cols), jnp.bfloat16)],
        compiler_params=params(32),
        cost_estimate=cost(4 * rows * width * cols, 4 * width * cols + 4 * rows * width),
        name="keys_values",
    )(
        table, *[x for side in xs for x in side], *gains,
        *[in_hbm(wk)] * sides, *[in_hbm(wv)] * sides,
        kgain, cosine, sine,
    )


def q_kernel(sides, table, *refs):
    normed, wqs = refs[:sides], refs[sides : 2 * sides]
    qgain, cosine, sine, out = refs[2 * sides :]
    head = qgain.shape[1]
    lin = summed_dot(normed, wqs)
    gains = qgain[...].astype(jnp.float32)
    for h in range(lin.shape[1] // head):
        out[:, h * head : (h + 1) * head] = head_norm_rope(
            lin[:, h * head : (h + 1) * head], gains, cosine[...], sine[...]
        ).astype(jnp.bfloat16)


def make_q(lay, table, normed, wq, qgain, cosine, sine, part):
    sides = len(normed)
    rows = normed[0].shape[0]
    width, cols = wq.shape
    tile = 512 if cols % 512 == 0 else cols
    head = qgain.shape[1]
    fixed = lambda n, t: (0, 0)
    here = lambda n, t: (part, 0)
    weights = []
    for side in range(sides):
        index = half_index(lay, sides, side)
        weights.append(
            pl.BlockSpec(
                (normed[side].shape[1], tile), lambda n, t, index=index: (index(t), n)
            )
        )
    return pl.pallas_call(
        functools.partial(q_kernel, sides),
        grid_spec=pltpu.PrefetchScalarGridSpec(
            num_scalar_prefetch=1,
            grid=(cols // tile,),
            in_specs=[pl.BlockSpec(x.shape, fixed) for x in normed]
            + weights
            + [
                pl.BlockSpec((1, head), fixed),
                pl.BlockSpec((rows, head), here),
                pl.BlockSpec((rows, head), here),
            ],
            out_specs=pl.BlockSpec((rows, tile), lambda n, t: (0, n)),
        ),
        out_shape=jax.ShapeDtypeStruct((rows, cols), jnp.bfloat16),
        compiler_params=params(24),
        cost_estimate=cost(2 * rows * width * cols, 2 * width * cols + 2 * rows * (width + cols)),
        name="queries",
    )(table, *normed, *[in_hbm(wq)] * sides, qgain, cosine, sine)


def attention_kernel(lay, spans, most, per_kv, head, beside, owners, pages_each, table, *refs):
    q_refs = refs[:PARTS]
    kv_refs = refs[PARTS : PARTS + owners * PARTS]
    out, pages, keys, values, asked = refs[PARTS + owners * PARTS :]
    chips = lay.chips
    here, rows = kv_refs[0].shape[1], kv_refs[0].shape[2]
    group_rank = table[lay.group_rank]
    chip, core = lax.div(group_rank, CORES), lax.rem(group_rank, CORES)
    heads = range(beside)
    for p in range(PARTS):
        asked[p * here : (p + 1) * here] = q_refs[p][...]
    for o in range(owners):
        back, other = o // CORES, o % CORES
        owner = lax.rem(chip + chips - back, chips) * CORES + (core if other == 0 else 1 - core)
        at = pl.ds(pl.multiple_of(owner * rows, rows), rows)
        for p in range(PARTS):
            for i in range(here):
                k = table[lay.origin + o * spans + p * here + i]
                for h in heads:
                    lanes = slice(h * head, (h + 1) * head)
                    keys[h, k, at] = kv_refs[o * PARTS + p][0, i, :, lanes]
                    values[h, k, at] = kv_refs[o * PARTS + p][1, i, :, lanes]

    for i in range(pages_each):
        page = table[lay.page + group_rank * pages_each + i]
        k = lax.div(page, pages_each)
        at = pl.ds(pl.multiple_of(lax.rem(page, pages_each) * PAGE_ROWS, PAGE_ROWS), PAGE_ROWS)
        for h in heads:
            lanes = slice(h * head, (h + 1) * head)
            pages[i, 0, :, lanes] = keys[h, k, at]
            pages[i, 1, :, lanes] = values[h, k, at]

    scale = (1.0 / math.sqrt(head)) * math.log2(math.e)
    q_rows, k_rows = per_kv * rows, owners * rows
    row = lax.broadcasted_iota(jnp.int32, (q_rows, k_rows), 0)
    col = lax.broadcasted_iota(jnp.int32, (q_rows, k_rows), 1)
    allowed = col <= group_rank * rows + row % rows

    def one_place(place, carry):
        k = table[lay.span_at + place]
        earlier = table[lay.earlier_at + place]

        def with_earlier(count):
            scores = [[] for _ in heads]
            for h in heads:
                queries = jnp.concatenate(
                    [
                        asked[place, :, (h * per_kv + g) * head : (h * per_kv + g + 1) * head]
                        for g in range(per_kv)
                    ],
                    axis=0,
                )
                for back in range(count + 1):
                    s = lax.dot_general(
                        queries, keys[h, k - back], (((1,), (1,)), ((), ())),
                        preferred_element_type=jnp.float32,
                    )
                    if back == 0:
                        s = jnp.where(allowed, s, very_negative)
                    scores[h].append(s)
            for h in heads:
                best = functools.reduce(jnp.maximum, scores[h])
                best = jnp.max(best, axis=-1, keepdims=True)
                shifted = best * scale
                weights = [jnp.exp2(s * scale - shifted) for s in scores[h]]
                total = jnp.sum(
                    functools.reduce(lambda a, b: a + b, weights), axis=-1, keepdims=True
                )
                summed = None
                for back, w in enumerate(weights):
                    term = jnp.dot(
                        w.astype(jnp.bfloat16), values[h, k - back],
                        preferred_element_type=jnp.float32,
                    )
                    summed = term if summed is None else summed + term
                result = (summed / total).astype(jnp.bfloat16)
                for g in range(per_kv):
                    at = (h * per_kv + g) * head
                    out[place, :, at : at + head] = result[g * rows : (g + 1) * rows]

        for count in range(most):
            pl.when(earlier == count)(functools.partial(with_earlier, count))
        return carry

    lax.fori_loop(0, spans, one_place, 0)


def make_attention(lay, most, table, queries, gathered, per_kv, head, pages_each, first, count):
    here, rows, cols = queries[0].shape
    spans = here * PARTS
    owners = len(gathered)
    at = first // count
    q_spec = pl.BlockSpec((here, rows, count * per_kv * head), lambda h, t: (0, 0, at + h))
    kv_spec = pl.BlockSpec((2, here, rows, count * head), lambda h, t: (0, 0, 0, at + h))
    flat = [x for origin in gathered for x in origin]
    all_rows = spans * rows
    pairs = 2.2 * all_rows * owners * rows * per_kv * count
    return pl.pallas_call(
        functools.partial(
            attention_kernel, lay, spans, most, per_kv, head, count, owners, pages_each
        ),
        grid_spec=pltpu.PrefetchScalarGridSpec(
            num_scalar_prefetch=1,
            grid=(1,),
            in_specs=[q_spec] * PARTS + [kv_spec] * len(flat),
            out_specs=[
                pl.BlockSpec((spans, rows, count * per_kv * head), lambda h, t: (0, 0, h)),
                pl.BlockSpec((pages_each, 2, PAGE_ROWS, count * head), lambda h, t: (0, 0, 0, h)),
            ],
            scratch_shapes=[pltpu.VMEM((count, spans, owners * rows, head), jnp.bfloat16)] * 2
            + [pltpu.VMEM((spans, rows, count * per_kv * head), jnp.bfloat16)],
        ),
        out_shape=[
            jax.ShapeDtypeStruct((spans, rows, count * per_kv * head), jnp.bfloat16),
            jax.ShapeDtypeStruct((pages_each, 2, PAGE_ROWS, count * head), jnp.bfloat16),
        ],
        compiler_params=params(32),
        cost_estimate=cost(
            4 * pairs * head, 4 * all_rows * cols + 2 * len(flat) * flat[0].size, pairs
        ),
        name="attention",
    )(table, *queries, *flat)


def project_kernel(pieces, follows, tile, table, *refs):
    attended, wo, outs = refs[:pieces], refs[pieces], refs[pieces + 1 + follows :]
    total, at = None, 0
    for piece in attended:
        depth = piece.shape[1]
        term = jnp.dot(piece[...], wo[at : at + depth], preferred_element_type=jnp.float32)
        total = term if total is None else total + term
        at += depth
    total = total.astype(jnp.bfloat16)
    step = 0
    for out in outs:
        for at in range(0, out.shape[1], tile):

            @pl.when(pl.program_id(0) == step)
            def _(out=out, at=at):
                out[:, at : at + tile] = total

            step += 1


def make_projection(lay, table, attended, wo, tile, first, widths, name, follows=()):
    rows = attended[0].shape[0]
    depth = wo.shape[0]
    count = sum(widths)
    return pl.pallas_call(
        functools.partial(project_kernel, len(attended), len(follows), tile),
        grid_spec=pltpu.PrefetchScalarGridSpec(
            num_scalar_prefetch=1,
            grid=(count,),
            in_specs=[pl.BlockSpec(x.shape, lambda n, t: (0, 0)) for x in attended]
            + [pl.BlockSpec((depth, tile), lambda n, t: (0, first(t[lay.tensor_rank]) + n))]
            + [pl.BlockSpec(memory_space=pl.ANY)] * len(follows),
            out_specs=[pl.BlockSpec((rows, w * tile), lambda n, t: (0, 0)) for w in widths],
        ),
        out_shape=[jax.ShapeDtypeStruct((rows, w * tile), jnp.bfloat16) for w in widths],
        compiler_params=params(20),
        cost_estimate=cost(
            2 * rows * depth * count * tile, 2 * (rows * depth + (rows + depth) * count * tile)
        ),
        name=name,
    )(table, *attended, in_hbm(wo), *follows)


def add_kernel(lay, blocks, table, *refs):
    x_refs, own, received = refs[:blocks], refs[blocks], refs[blocks + 1]
    outs, moved = refs[blocks + 2 : -1], refs[-1]
    rows = moved.shape[1]
    place = 0
    for x in x_refs:
        for at in range(0, x.shape[0], rows):
            summed = own[place].astype(jnp.float32) + received[place].astype(jnp.float32)
            moved[table[lay.sent_as + place]] = (
                x[at : at + rows].astype(jnp.float32) + summed
            ).astype(jnp.bfloat16)
            place += 1
    for n, out in enumerate(outs):
        for flip in range(CORES):
            out[flip] = moved[n * CORES + flip]


def make_sum(lay, table, arrived, own, received, first):
    spans, rows, cols = received.shape
    chunk = first // cols
    whole = lambda n, t: (0, 0, 0)
    return pl.pallas_call(
        functools.partial(add_kernel, lay, len(arrived)),
        grid_spec=pltpu.PrefetchScalarGridSpec(
            num_scalar_prefetch=1,
            grid=(1,),
            in_specs=[pl.BlockSpec((x.shape[0], cols), lambda n, t: (0, chunk)) for x in arrived]
            + [pl.BlockSpec((spans, rows, cols), whole)] * 2,
            out_specs=[pl.BlockSpec((CORES, rows, cols), whole)] * lay.chips,
            scratch_shapes=[pltpu.VMEM((spans, rows, cols), jnp.bfloat16)],
        ),
        out_shape=[jax.ShapeDtypeStruct((CORES, rows, cols), jnp.bfloat16)] * lay.chips,
        compiler_params=params(12),
        cost_estimate=cost(3 * spans * rows * cols, 8 * spans * rows * cols),
        name="residual",
    )(table, *arrived, own, received)


def place_kernel(lay, chunks, table, *refs):
    out = refs[-1]
    chips = lay.chips
    group_rank = table[lay.group_rank]
    chip, core = lax.div(group_rank, CORES), lax.rem(group_rank, CORES)
    first = 0
    for c in range(chunks):
        same, swapped = refs[c * (chips + 1) : (c + 1) * (chips + 1) - 1], refs[(c + 1) * (chips + 1) - 1]
        rows, cols = swapped.shape[1:]
        for n, hop in enumerate(hop_order(chips)):
            owner = lax.rem(chip + chips - hop, chips) * CORES
            for block, at_core in ((same[n][0], core), (swapped[n], 1 - core)):
                at = pl.multiple_of((owner + at_core) * rows, rows)
                out[pl.ds(at, rows), first : first + cols] = block
        first += cols


def make_placed(lay, table, pieces, cols):
    flat = [x for same, swapped in pieces for x in [*same, swapped]]
    chips, rows, _ = pieces[0][1].shape
    shape = (chips * CORES * rows, cols)
    return pl.pallas_call(
        functools.partial(place_kernel, lay, len(pieces)),
        grid_spec=pltpu.PrefetchScalarGridSpec(
            num_scalar_prefetch=1,
            grid=(1,),
            in_specs=[pl.BlockSpec(x.shape, lambda n, t: (0, 0, 0)) for x in flat],
            out_specs=pl.BlockSpec(shape, lambda n, t: (0, 0)),
        ),
        out_shape=jax.ShapeDtypeStruct(shape, jnp.bfloat16),
        compiler_params=params(16),
        cost_estimate=cost(0, 4 * shape[0] * shape[1]),
        name="placed",
    )(table, *flat)


def rope_tables(earlier, span_len, first_row, rows, head):
    half = head // 2
    freqs = jnp.power(
        jnp.float32(rope_base), -jnp.arange(half, dtype=jnp.float32) * 2.0 / head
    )
    at = earlier[:, None] * span_len + first_row + jnp.arange(rows, dtype=jnp.int32)[None, :]
    angles = at.reshape(-1).astype(jnp.float32)[:, None] * freqs[None, :]
    cosine, sine = jnp.cos(angles), jnp.sin(angles)
    return (
        jnp.concatenate([cosine, cosine], axis=1),
        jnp.concatenate([-sine, sine], axis=1),
    )


def after(x, done):
    return lax.optimization_barrier((x, done))[0]


def shift(x, owners, hop, flip):
    chips = owners // CORES
    pairs = [
        (z * CORES + c, (z + hop) % chips * CORES + (c ^ flip))
        for z in range(chips)
        for c in range(CORES)
    ]
    return lax.ppermute(x, "group", pairs)


def local(
    hidden_in, ln_gain, wq, wk, wv, q_gain, key_norm_gain, wo,
    prompt_spans, span_source, span_target, page_slot,
):
    _, span_len, cols = hidden_in.shape
    tensor_size = lax.axis_size("tensor")
    owners = lax.axis_size("group")
    tensor_rank = lax.axis_index("tensor")
    group_rank = lax.axis_index("group")
    chips = owners // CORES
    head = q_gain.shape[0]
    rows = span_len // owners
    pages_each = span_len // PAGE_ROWS
    spans = span_source.shape[0]
    here = spans // PARTS
    most = min(spans - (prompt_spans.shape[0] - 1), spans // 2)
    kv_cols = wk.shape[1]
    paired = tensor_size == 2
    swap = [(0, 1), (1, 0)]
    lay = Layout(spans, spans * pages_each, owners)

    if kv_cols < head:
        share = head // kv_cols
        sets = [list(range(i, i + share)) for i in range(0, tensor_size, share)]
        wk, wv = [
            lax.all_gather(w, "tensor", axis=1, tiled=True, axis_index_groups=sets)
            for w in (wk, wv)
        ]
    per_kv = wq.shape[1] // max(head, wk.shape[1])

    chip, core = group_rank // CORES, group_rank % CORES
    split = hidden_in.reshape(owners, rows, cols)

    def rows_for(hop, flip):
        to = lax.rem(chip + hop, chips) * CORES + lax.rem(core + flip, CORES)
        return lax.dynamic_index_in_dim(split, to, 0, keepdims=False)

    cross = lambda x: lax.ppermute(x, "tensor", swap)

    hops = hop_order(chips)
    paired_hops = hops[2:]
    near = [rows_for(hop, flip) for hop in hops[1:2] for flip in range(CORES)]
    near = [shift(x, owners, hops[1], flip) for flip, x in enumerate(near)]
    swapped = shift(
        jnp.stack([rows_for(hop, 1) for hop in hops[:1] + paired_hops]), owners, 0, 1
    )
    arrived = [rows_for(0, 0), swapped[0]] + near
    moves = []
    for n, hop in enumerate(paired_hops):
        pair = [rows_for(hop, 0), swapped[1 + n]]
        if n < len(paired_hops) - 1:
            moves.append((hop, jnp.concatenate(pair)))
        else:
            moves += [(hop, block) for block in pair]

    ranks = jnp.stack([group_rank, tensor_rank]).astype(jnp.int32)
    table = make_tables(
        lay, spans, spans * pages_each, ranks, prompt_spans, span_source, span_target, page_slot
    )
    earlier = table[lay.earlier_at : lay.earlier_at + spans]
    cosine, sine = rope_tables(earlier, span_len, group_rank * rows, rows, head)

    crossed = [cross(x) for x in arrived] if paired else []
    if paired:
        gain = ln_gain[None]
        gains = [gain, cross(after(gain, swapped))]
    else:
        gains = [lax.all_gather(ln_gain, "tensor", axis=0, tiled=True)[None]]

    kvs, norms = [], []

    def make_part(own_rows, crossed_rows):
        if paired:
            xs = [own_rows, [in_hbm(x) for x in crossed_rows]]
        else:
            xs = [[lax.all_gather(jnp.concatenate(own_rows), "tensor", axis=1, tiled=True)]]
        *normed, kv = make_kv(
            lay, table, xs, gains, wk, wv, key_norm_gain[None], cosine, sine, len(kvs)
        )
        kvs.append([kv.reshape(2, here, rows, kv.shape[2])])
        norms.append(normed)

    def one_back(p, done=()):
        kvs[p].append(shift(after(kvs[p][-1], done), owners, 1, 0))

    begun = 0
    for n in range(len(moves) + 1):
        if n:
            hop, block = moves[n - 1]
            if paired:
                landed = arrived[-1:] if n > 1 else near
                matching = crossed[2 * n - 2 : 2 * n] if n < 3 else crossed[n + 1]
                block = after(block, (landed, matching, gains))
            arrived.append(shift(block, owners, hop, 0))
            if paired:
                block = arrived[-1]
                if n == len(moves) and kvs:
                    block = after(block, kvs[0][0])
                crossed.append(cross(block))
        if sum(x.shape[0] for x in arrived[begun:]) == here * rows:
            make_part(arrived[begun:], crossed[begun:])
            begun = len(arrived)
            for _ in range(min(2, chips - 1) if len(kvs) == 1 else min(1, chips - 1)):
                one_back(len(kvs) - 1)

    queries, done = [], kvs[1][0]
    for p in range(PARTS):
        made = make_q(
            lay, table, norms[p], wq, after(q_gain[None], done), cosine, sine, p
        )
        queries.append(made.reshape(here, rows, made.shape[1]))
        done = queries[-1]
    for p in range(PARTS):
        while len(kvs[p]) < chips:
            one_back(p, queries[p])
    gathered = []
    for back in range(chips):
        gathered.append([kv[back] for kv in kvs])
        gathered.append([shift(kv[back], owners, 0, 1) for kv in kvs])

    own_kv = wk.shape[1] // head
    sets = [own_kv // 2] * 2 if own_kv % 2 == 0 else [1] * own_kv
    attended, pages, first = [], [], 0
    for count in sets:
        made, cut = make_attention(
            lay, most, table, queries, gathered, per_kv, head, pages_each, first, count
        )
        attended.append(made.reshape(spans * rows, -1))
        pages.append(cut)
        first += count

    if paired:
        tile = 512 if cols % 512 == 0 else cols
        tiles = cols // tile
        widths = [2, 2, 1] if tiles == 5 else [tiles]
        others = [cross(pages[0])]
        project = functools.partial(make_projection, lay, table, attended, wo, tile)
        send = project(lambda r: (1 - r) * tiles, widths[:1], "send_part", (others[0],))
        if widths[1:]:
            send += project(
                lambda r: (1 - r) * tiles + widths[0], widths[1:], "send_part", (send[0],)
            )
        own = project(lambda r: r * tiles, widths, "own_part", (send[-1],))
        pieces, received, landed, first = [], [], [], 0
        for n, sent in enumerate(send):
            if n:
                sent = after(sent, (received[-1], own, landed[-2:-1]))
            received.append(cross(sent))
            moved = make_sum(
                lay, table, arrived, own[n].reshape(spans, rows, -1),
                received[-1].reshape(spans, rows, -1), first,
            )
            same = [
                shift(x, owners, hop, 0) if hop else x
                for hop, x in zip(hop_order(chips), moved)
            ]
            landed.append(same)
            swapped = shift(jnp.concatenate([x[1:] for x in same]), owners, 0, 1)
            pieces.append((same, swapped))
            first += sent.shape[1]
        mixed = make_placed(lay, table, pieces, cols).reshape(1, span_len, cols)
        for cut in pages[1:]:
            others.append(cross(after(cut, received[-1])))
        low = [jnp.where(tensor_rank == 0, a, b) for a, b in zip(pages, others)]
        high = [jnp.where(tensor_rank == 0, b, a) for a, b in zip(pages, others)]
        cache = jnp.concatenate(low + high, axis=3)
    else:
        pages = jnp.concatenate(pages, axis=3)
        attended = jnp.concatenate(attended, axis=1)
        if kv_cols < head:
            pages = lax.dynamic_slice_in_dim(
                pages, lax.rem(tensor_rank, head // kv_cols) * kv_cols, kv_cols, 3
            )
        cache = lax.all_gather(pages, "tensor", axis=3, tiled=True)
        partial = jnp.dot(attended, wo, preferred_element_type=jnp.float32)
        summed = lax.psum_scatter(
            partial.astype(jnp.bfloat16), "tensor", scatter_dimension=1, tiled=True
        )
        summed = summed.reshape(spans, rows, cols).astype(jnp.float32)
        x = jnp.concatenate(arrived).reshape(spans, rows, cols).astype(jnp.float32)
        moved = (x + summed).astype(jnp.bfloat16)
        targets = table[lay.target_at : lay.target_at + spans]
        moved = jnp.zeros_like(moved).at[targets].set(moved, unique_indices=True)
        moved = lax.all_to_all(moved, "group", split_axis=0, concat_axis=0, tiled=True)
        mixed = moved.reshape(1, span_len, cols)
    return (mixed, cache)


def solution(mesh):
    in_specs = (
        P(("replica", "group"), None, "tensor"),
        P("tensor"),
        P(None, "tensor"),
        P(None, "tensor"),
        P(None, "tensor"),
        P(),
        P(),
        P("tensor", None),
        P("replica"),
        P("replica"),
        P("replica"),
        P("replica"),
    )
    out_specs = (P(("replica", "group"), None, "tensor"), P(("replica", "group"), None, None, None))
    return jax.shard_map(local, mesh=mesh, in_specs=in_specs, out_specs=out_specs, check_vma=False)
```

profile of v0, /device:TPU:0, one launch (start us, length us, event | category | flops | bytes accessed | tf_op | source)
XLA Modules:
  0.0 287.1 jit_solution(17157147844983650975)
XLA Ops:
  0.7 1.9 dynamic-slice_bitcast_fusion
  3.3 2.7 collective-permute-start.2
  6.0 1.6 collective-permute-start.1
  7.6 1.5 collective-permute-start.3
  10.5 1.5 collective-permute-start.4
  12.1 4.0 %collective-permute-done.2.refs_3_ = bf16[64,2560]{1,0:T(8,128)(2,1)S(1)} collective-permute-done((bf16[64,2560]{1,0:T(8,128)(2,1)S(1)}, bf16[64,2560]{1,0:T(8,128)(2,1)S(1)}, u32[]{:S(2)}, u32[]{:S(2)}) %collective-permute-start.2) | collective-permute-done | bytes 327712 | tf_op jit(solution)/shard_map/ppermute | solution.py:524
  16.0 7.3 %collective-permute-done.1.refs_2_ = bf16[64,2560]{1,0:T(8,128)(2,1)S(1)} collective-permute-done((bf16[64,2560]{1,0:T(8,128)(2,1)S(1)}, bf16[64,2560]{1,0:T(8,128)(2,1)S(1)}, u32[]{:S(2)}, u32[]{:S(2)}) %collective-permute-start.1) | collective-permute-done | bytes 327712 | tf_op jit(solution)/shard_map/ppermute | solution.py:524
  25.0 2.2 collective-permute-start.6
  27.2 1.5 collective-permute-start.8
  29.2 12.0 %collective-permute-done.6.refs_0_.refs_4_ = bf16[128,2560]{1,0:T(8,128)(2,1)S(1)} collective-permute-done((bf16[128,2560]{1,0:T(8,128)(2,1)S(1)}, bf16[128,2560]{1,0:T(8,128)(2,1)S(1)}, u32[]{:S(2)}, u32[]{:S(2)}) %collective-permute-start.6) | collective-permute-done | bytes 655392 | tf_op jit(solution)/shard_map/ppermute | solution.py:524
  41.3 1.3 collective-permute-start.10
  42.7 1.4 tables.1.table
  45.4 14.7 %collective-permute-done.9.refs_1_.refs_5_ = bf16[64,2560]{1,0:T(8,128)(2,1)S(1)} collective-permute-done((bf16[64,2560]{1,0:T(8,128)(2,1)S(1)}, bf16[64,2560]{1,0:T(8,128)(2,1)S(1)}, u32[]{:S(2)}, u32[]{:S(2)}) %collective-permute-start.9) | collective-permute-done | bytes 327712 | tf_op jit(solution)/shard_map/ppermute | solution.py:524
  62.1 8.7 %keys_values.2 = (bf16[256,2560]{1,0:T(8,128)(2,1)S(1)}, bf16[256,2560]{1,0:T(8,128)(2,1)S(1)}, bf16[2,256,512]{2,1,0:T(8,128)(2,1)S(1)}) custom-call(s32[130]{0:T(256)S(1)} %tables.1.table, bf16[64,2560]{1,0:T(8,128)(2,1)S(1)} %get-tuple-element.89.refs_0_, bf16[64,2560]{1,0:T(8,128)(2,1)S(1)} %get-tuple-element.96.refs_1_, ...), custom_call_target="tpu_custom_call" | custom-call | flops 53687092 | bytes 314572 | tf_op jit(solution)/shard_map/keys_values/pallas_call | solution.py:180
  71.7 5.8 %collective-permute-done.11.refs_2_.refs_6_ = bf16[64,2560]{1,0:T(8,128)(2,1)S(1)} collective-permute-done((bf16[64,2560]{1,0:T(8,128)(2,1)}, bf16[64,2560]{1,0:T(8,128)(2,1)S(1)}, u32[]{:S(2)}, u32[]{:S(2)}) %collective-permute-start.11) | collective-permute-done | bytes 327712 | tf_op jit(solution)/shard_map/ppermute | solution.py:524
  78.4 1.9 collective-permute-done.12.refs_4_
  80.3 6.9 %collective-permute-done.13.refs_5_ = bf16[64,2560]{1,0:T(8,128)(2,1)S(1)} collective-permute-done((bf16[64,2560]{1,0:T(8,128)(2,1)S(1)}, bf16[64,2560]{1,0:T(8,128)(2,1)S(1)}, u32[]{:S(2)}, u32[]{:S(2)}) %collective-permute-start.13) | collective-permute-done | bytes 327712 | tf_op jit(solution)/shard_map/ppermute | solution.py:564
  88.0 8.7 %keys_values.3 = (bf16[256,2560]{1,0:T(8,128)(2,1)S(1)}, bf16[256,2560]{1,0:T(8,128)(2,1)S(1)}, bf16[2,256,512]{2,1,0:T(8,128)(2,1)S(1)}) custom-call(s32[130]{0:T(256)S(1)} %tables.1.table, bf16[128,2560]{1,0:T(8,128)(2,1)S(1)} %collective-permute-done.6.refs_0_.refs_4_, bf16[64,2560]{1,0:T(8,128)(2,1)S(1)} %collective-permute-done.9.refs_1_.refs_5_, ...), custom_call_target="tpu_custom_call" | custom-call | flops 53687092 | bytes 314572 | tf_op jit(solution)/shard_map/keys_values/pallas_call | solution.py:180
  96.7 2.1 collective-permute-start.17
  99.9 11.3 %queries.2 = bf16[256,2048]{1,0:T(8,128)(2,1)S(1)} custom-call(s32[130]{0:T(256)S(1)} %tables.1.table, bf16[256,2560]{1,0:T(8,128)(2,1)S(1)} %get-tuple-element.46.refs_0_, bf16[256,2560]{1,0:T(8,128)(2,1)S(1)} %get-tuple-element.47.refs_1_, bf16[5120,2048]{1,0:T(8,128)(2,1)} %refs_3_.3, bf16[5120,2048]{1,0:T(8,128)(2,1)} %refs_3_.3, ...), custom_call_target="tpu_custom_call" | custom-call | flops 107374184 | bytes 492830 | tf_op jit(solution)/shard_map/queries/pallas_call | solution.py:237
  111.2 11.3 %queries.3 = bf16[256,2048]{1,0:T(8,128)(2,1)S(1)} custom-call(s32[130]{0:T(256)S(1)} %tables.1.table, bf16[256,2560]{1,0:T(8,128)(2,1)S(1)} %get-tuple-element.52.refs_0_, bf16[256,2560]{1,0:T(8,128)(2,1)S(1)} %get-tuple-element.53.refs_1_, bf16[5120,2048]{1,0:T(8,128)(2,1)} %refs_3_.3, bf16[5120,2048]{1,0:T(8,128)(2,1)} %refs_3_.3, ...), custom_call_target="tpu_custom_call" | custom-call | flops 107374184 | bytes 492830 | tf_op jit(solution)/shard_map/queries/pallas_call | solution.py:237
  123.3 1.6 collective-permute-start.24
  124.9 14.4 %collective-permute-done.21.refs_11_ = bf16[2,4,64,512]{3,2,1,0:T(8,128)(2,1)S(1)} collective-permute-done((bf16[2,4,64,512]{3,2,1,0:T(8,128)(2,1)S(1)}, bf16[2,4,64,512]{3,2,1,0:T(8,128)(2,1)S(1)}, u32[]{:S(2)}, u32[]{:S(2)}) %collective-permute-start.21) | collective-permute-done | bytes 524320 | tf_op jit(solution)/shard_map/ppermute | solution.py:524
  139.8 10.7 %collective-permute-done.24.refs_14_ = bf16[2,4,64,512]{3,2,1,0:T(8,128)(2,1)S(1)} collective-permute-done((bf16[2,4,64,512]{3,2,1,0:T(8,128)(2,1)S(1)}, bf16[2,4,64,512]{3,2,1,0:T(8,128)(2,1)S(1)}, u32[]{:S(2)}, u32[]{:S(2)}) %collective-permute-start.24) | collective-permute-done | bytes 524320 | tf_op jit(solution)/shard_map/ppermute | solution.py:524
  151.0 7.6 %collective-permute-done.25.refs_15_ = bf16[2,4,64,512]{3,2,1,0:T(8,128)(2,1)S(1)} collective-permute-done((bf16[2,4,64,512]{3,2,1,0:T(8,128)(2,1)S(1)}, bf16[2,4,64,512]{3,2,1,0:T(8,128)(2,1)S(1)}, u32[]{:S(2)}, u32[]{:S(2)}) %collective-permute-start.25) | collective-permute-done | bytes 524320 | tf_op jit(solution)/shard_map/ppermute | solution.py:524
  158.7 1.9 collective-permute-done.27.refs_17_
  160.6 10.3 %attention.2 = (bf16[8,64,1024]{2,1,0:T(8,128)(2,1)S(1)}, bf16[4,2,128,256]{3,2,1,0:T(8,128)(2,1)S(1)}) custom-call(s32[130]{0:T(256)S(1)} %tables.1.table, bf16[4,64,2048]{2,1,0:T(8,128)(2,1)S(1)} %bitcast.40, bf16[4,64,2048]{2,1,0:T(8,128)(2,1)S(1)} %bitcast.42, bf16[2,4,64,512]{3,2,1,0:T(8,128)(2,1)S(1)} %bitcast.46, ...), custom_call_target="tpu_custom_call" | custom-call | flops 47244640 | bytes 251658 | tf_op jit(solution)/shard_map/attention/pallas_call | solution.py:355
  170.9 1.5 collective-permute-start.28
  172.4 11.0 %attention.3 = (bf16[8,64,1024]{2,1,0:T(8,128)(2,1)S(1)}, bf16[4,2,128,256]{3,2,1,0:T(8,128)(2,1)}) custom-call(s32[130]{0:T(256)S(1)} %tables.1.table, bf16[4,64,2048]{2,1,0:T(8,128)(2,1)S(1)} %bitcast.41, bf16[4,64,2048]{2,1,0:T(8,128)(2,1)S(1)} %bitcast.43, bf16[2,4,64,512]{3,2,1,0:T(8,128)(2,1)S(1)} %bitcast.47, bf16[2,4,64,512]{3,2,1,0:T(8,128)(2,1)S(1)} %bitcast.51, ...), custom_call_target="tpu_custom_call" | custom-call | flops 47244640 | bytes 251658 | tf_op jit(solution)/shard_map/attention/pallas_call | solution.py:355
  183.4 1.5 collective-permute-done.28.refs_3_
  184.9 4.8 %send_part.2.refs_3_ = bf16[512,1024]{1,0:T(8,128)(2,1)S(1)} custom-call(s32[130]{0:T(256)S(1)} %tables.1.table, bf16[512,1024]{1,0:T(8,128)(2,1)S(1)} %bitcast.34, bf16[512,1024]{1,0:T(8,128)(2,1)S(1)} %bitcast.37, bf16[2048,5120]{1,0:T(8,128)(2,1)} %refs_2_.9, bf16[4,2,128,256]{3,2,1,0:T(8,128)(2,1)S(1)} %collective-permute-done.28.refs_3_), custom_call_target="tpu_custom_call" | custom-call | flops 42949672 | bytes 146800 | tf_op jit(solution)/shard_map/send_part/pallas_call | solution.py:406
  189.7 1.5 collective-permute-start.29
  191.2 6.4 %send_part.3 = (bf16[512,1024]{1,0:T(8,128)(2,1)S(1)}, bf16[512,512]{1,0:T(8,128)(2,1)S(1)}) custom-call(s32[130]{0:T(256)S(1)} %tables.1.table, bf16[512,1024]{1,0:T(8,128)(2,1)S(1)} %bitcast.35, bf16[512,1024]{1,0:T(8,128)(2,1)S(1)} %bitcast.38, bf16[2048,5120]{1,0:T(8,128)(2,1)} %refs_2_.9, bf16[512,1024]{1,0:T(8,128)(2,1)S(1)} %send_part.2.refs_3_), custom_call_target="tpu_custom_call" | custom-call | flops 64424508 | bytes 199229 | tf_op jit(solution)/shard_map/send_part/pallas_call | solution.py:406
  197.6 9.5 %own_part.1 = (bf16[512,1024]{1,0:T(8,128)(2,1)S(1)}, bf16[512,1024]{1,0:T(8,128)(2,1)S(1)}, bf16[512,512]{1,0:T(8,128)(2,1)S(1)}) custom-call(s32[130]{0:T(256)S(1)} %tables.1.table, bf16[512,1024]{1,0:T(8,128)(2,1)S(1)} %bitcast.36, bf16[512,1024]{1,0:T(8,128)(2,1)S(1)} %bitcast.39, bf16[2048,5120]{1,0:T(8,128)(2,1)} %refs_2_.9, ...), custom_call_target="tpu_custom_call" | custom-call | flops 107374184 | bytes 304087 | tf_op jit(solution)/shard_map/own_part/pallas_call | solution.py:406
  207.1 7.0 %collective-permute-done.29 = bf16[512,1024]{1,0:T(8,128)(2,1)S(1)} collective-permute-done((bf16[512,1024]{1,0:T(8,128)(2,1)S(1)}, bf16[512,1024]{1,0:T(8,128)(2,1)S(1)}, u32[]{:S(2)}, u32[]{:S(2)}) %collective-permute-start.29) | collective-permute-done | bytes 1048608 | tf_op jit(solution)/shard_map/ppermute | solution.py:564
  214.1 1.5 collective-permute-start.34
  216.8 3.8 %collective-permute-start.31 = (bf16[2,64,1024]{2,1,0:T(8,128)(2,1)S(1)}, bf16[2,64,1024]{2,1,0:T(8,128)(2,1)S(1)}, u32[]{:S(2)}, u32[]{:S(2)}) collective-permute-start(bf16[2,64,1024]{2,1,0:T(8,128)(2,1)S(1)} %get-tuple-element.65), channel_id=1, source_target_pairs={{0,6},{1,7},{2,0},{3,1},{4,2},{5,3},{6,4},{7,5},{8,14},{9,15},{10,... | collective-permute-start | bytes 786440 | tf_op jit(solution)/shard_map/ppermute | solution.py:524
  220.6 7.2 %collective-permute-done.30.refs_1_ = bf16[2,64,1024]{2,1,0:T(8,128)(2,1)S(1)} collective-permute-done((bf16[2,64,1024]{2,1,0:T(8,128)(2,1)S(1)}, bf16[2,64,1024]{2,1,0:T(8,128)(2,1)S(1)}, u32[]{:S(2)}, u32[]{:S(2)}) %collective-permute-start.30) | collective-permute-done | bytes 262176 | tf_op jit(solution)/shard_map/ppermute | solution.py:524
  227.8 2.3 collective-permute-done.31.refs_2_
  230.1 9.6 %collective-permute-done.32.refs_3_ = bf16[2,64,1024]{2,1,0:T(8,128)(2,1)S(1)} collective-permute-done((bf16[2,64,1024]{2,1,0:T(8,128)(2,1)S(1)}, bf16[2,64,1024]{2,1,0:T(8,128)(2,1)S(1)}, u32[]{:S(2)}, u32[]{:S(2)}) %collective-permute-start.32) | collective-permute-done | bytes 262176 | tf_op jit(solution)/shard_map/ppermute | solution.py:524
  241.7 3.8 %collective-permute-start.36 = (bf16[2,64,1024]{2,1,0:T(8,128)(2,1)S(1)}, bf16[2,64,1024]{2,1,0:T(8,128)(2,1)S(1)}, u32[]{:S(2)}, u32[]{:S(2)}) collective-permute-start(bf16[2,64,1024]{2,1,0:T(8,128)(2,1)S(1)} %get-tuple-element.73), channel_id=1, source_target_pairs={{0,6},{1,7},{2,0},{3,1},{4,2},{5,3},{6,4},{7,5},{8,14},{9,15},{10,... | collective-permute-start | bytes 786440 | tf_op jit(solution)/shard_map/ppermute | solution.py:524
  245.6 5.9 %collective-permute-done.39 = bf16[512,512]{1,0:T(8,128)(2,1)S(1)} collective-permute-done((bf16[512,512]{1,0:T(8,128)(2,1)S(1)}, bf16[512,512]{1,0:T(8,128)(2,1)S(1)}, u32[]{:S(2)}, u32[]{:S(2)}) %collective-permute-start.39) | collective-permute-done | bytes 524320 | tf_op jit(solution)/shard_map/ppermute | solution.py:564
  251.5 1.5 residual.5
  255.8 12.1 %collective-permute-done.37.refs_8_ = bf16[2,64,1024]{2,1,0:T(8,128)(2,1)S(1)} collective-permute-done((bf16[2,64,1024]{2,1,0:T(8,128)(2,1)S(1)}, bf16[2,64,1024]{2,1,0:T(8,128)(2,1)S(1)}, u32[]{:S(2)}, u32[]{:S(2)}) %collective-permute-start.37) | collective-permute-done | bytes 262176 | tf_op jit(solution)/shard_map/ppermute | solution.py:524
  271.4 3.9 %collective-permute-done.41.refs_12_ = bf16[2,64,512]{2,1,0:T(8,128)(2,1)S(1)} collective-permute-done((bf16[2,64,512]{2,1,0:T(8,128)(2,1)}, bf16[2,64,512]{2,1,0:T(8,128)(2,1)S(1)}, u32[]{:S(2)}, u32[]{:S(2)}) %collective-permute-start.41) | collective-permute-done | bytes 131104 | tf_op jit(solution)/shard_map/ppermute | solution.py:524
  277.0 3.4 %placed.1 = bf16[512,2560]{1,0:T(8,128)(2,1)} custom-call(s32[130]{0:T(256)S(1)} %tables.1.table, bf16[2,64,1024]{2,1,0:T(8,128)(2,1)S(1)} %get-tuple-element.63.refs_0_, bf16[2,64,1024]{2,1,0:T(8,128)(2,1)S(1)} %copy-done.1, bf16[2,64,1024]{2,1,0:T(8,128)(2,1)S(1)} %copy-done.3, bf16[2,64,1024]{2,1,0:T(8,128)(2,1)S(1)} %copy-done.5, ...), custom_call_target="tpu_custom_call" | custom-call | bytes 104857 | tf_op jit(solution)/shard_map/placed/pallas_call | solution.py:484
  280.4 3.8 %collective-permute-done.44 = bf16[4,2,128,256]{3,2,1,0:T(8,128)(2,1)} collective-permute-done((bf16[4,2,128,256]{3,2,1,0:T(8,128)(2,1)}, bf16[4,2,128,256]{3,2,1,0:T(8,128)(2,1)}, u32[]{:S(2)}, u32[]{:S(2)}) %collective-permute-start.44) | collective-permute-done | bytes 524320 | tf_op jit(solution)/shard_map/ppermute | solution.py:564
  285.5 1.6 pad_maximum_fusion
  (151 shorter events, 25.4 us)
Async XLA Ops:
  2.6 40.0 %copy-start.19 = (s32[3]{0:T(128)S(1)}, s32[3]{0:T(128)}, u32[]{:S(2)}) copy-start(s32[3]{0:T(128)} %prompt_spans.1) | copy-start | bytes 40
  2.6 40.0 %copy-start.20 = (s32[8]{0:T(128)S(1)}, s32[8]{0:T(128)}, u32[]{:S(2)}) copy-start(s32[8]{0:T(128)} %source.1) | copy-start | bytes 100
  2.8 6.3 %collective-permute-start = (bf16[3,64,2560]{2,1,0:T(8,128)(2,1)S(1)}, bf16[3,64,2560]{2,1,0:T(8,128)(2,1)S(1)}, u32[]{:S(2)}, u32[]{:S(2)}) collective-permute-start(bf16[3,64,2560]{2,1,0:T(8,128)(2,1)S(1)} %pad_maximum_fusion.1), channel_id=1, source_target_pairs={{0,1},{1,0},{2,3},{3,2},{4,5},{5,4},{6,7},{7,6},{8,9},{9,8},{10,11... | collective-permute-start | bytes 2949128 | tf_op jit(solution)/shard_map/ppermute | solution.py:524
  3.3 12.7 %collective-permute-start.2 = (bf16[64,2560]{1,0:T(8,128)(2,1)S(1)}, bf16[64,2560]{1,0:T(8,128)(2,1)S(1)}, u32[]{:S(2)}, u32[]{:S(2)}) collective-permute-start(bf16[64,2560]{1,0:T(8,128)(2,1)S(1)} %get-tuple-element.84), channel_id=1, source_target_pairs={{0,3},{1,2},{2,5},{3,4},{4,7},{5,6},{6,1},{7,0},{8,11},{9,10},{10,... | collective-permute-start | bytes 983048 | tf_op jit(solution)/shard_map/ppermute | solution.py:524
  6.0 17.3 %collective-permute-start.1 = (bf16[64,2560]{1,0:T(8,128)(2,1)S(1)}, bf16[64,2560]{1,0:T(8,128)(2,1)S(1)}, u32[]{:S(2)}, u32[]{:S(2)}) collective-permute-start(bf16[64,2560]{1,0:T(8,128)(2,1)S(1)} %get-tuple-element.85), channel_id=1, source_target_pairs={{0,2},{1,3},{2,4},{3,5},{4,6},{5,7},{6,0},{7,1},{8,10},{9,11},{10,... | collective-permute-start | bytes 983048 | tf_op jit(solution)/shard_map/ppermute | solution.py:524
  7.6 15.7 %collective-permute-start.3 = (bf16[64,2560]{1,0:T(8,128)(2,1)S(1)}, bf16[64,2560]{1,0:T(8,128)(2,1)S(1)}, u32[]{:S(2)}, u32[]{:S(2)}) collective-permute-start(bf16[64,2560]{1,0:T(8,128)(2,1)S(1)} %get-tuple-element.89.refs_0_), channel_id=1, source_target_pairs={{0,8},{8,0},{1,9},{9,1},{2,10},{10,2},{3,11},{11,3},{4,12},{12,4},... | collective-permute-start | bytes 983048 | tf_op jit(solution)/shard_map/ppermute | solution.py:564
  9.1 53.0 %copy-start.17 = (bf16[128]{0:T(256)(128)(2,1)S(1)}, bf16[128]{0:T(256)(128)(2,1)}, u32[]{:S(2)}) copy-start(bf16[128]{0:T(256)(128)(2,1)} %param.18) | copy-start | bytes 772
  9.1 14.2 %collective-permute-start.5 = (bf16[1,2560]{1,0:T(2,128)(2,1)S(1)}, bf16[1,2560]{1,0:T(2,128)(2,1)S(1)}, u32[]{:S(2)}, u32[]{:S(2)}) collective-permute-start(bf16[1,2560]{1,0:T(2,128)(2,1)S(1)} %broadcast_in_dim.6.refs_8_.refs_6_), channel_id=1, source_target_pairs={{0,8},{8,0},{1,9},{9,1},{2,10},{10,2},{3,11},{11,3},{4,12},{12,4},... | collective-permute-start | bytes 15368 | tf_op jit(solution)/shard_map/ppermute | solution.py:564
  10.5 13.7 %collective-permute-start.4 = (bf16[64,2560]{1,0:T(8,128)(2,1)S(1)}, bf16[64,2560]{1,0:T(8,128)(2,1)S(1)}, u32[]{:S(2)}, u32[]{:S(2)}) collective-permute-start(bf16[64,2560]{1,0:T(8,128)(2,1)S(1)} %get-tuple-element.96.refs_1_), channel_id=1, source_target_pairs={{0,8},{8,0},{1,9},{9,1},{2,10},{10,2},{3,11},{11,3},{4,12},{12,4},... | collective-permute-start | bytes 983048 | tf_op jit(solution)/shard_map/ppermute | solution.py:564
  25.0 16.3 %collective-permute-start.6 = (bf16[128,2560]{1,0:T(8,128)(2,1)S(1)}, bf16[128,2560]{1,0:T(8,128)(2,1)S(1)}, u32[]{:S(2)}, u32[]{:S(2)}) collective-permute-start(bf16[128,2560]{1,0:T(8,128)(2,1)S(1)} %pad_maximum_fusion.2), channel_id=1, source_target_pairs={{0,6},{1,7},{2,0},{3,1},{4,2},{5,3},{6,4},{7,5},{8,14},{9,15},{10,... | collective-permute-start | bytes 1966088 | tf_op jit(solution)/shard_map/ppermute | solution.py:524
  27.2 16.9 %collective-permute-start.8 = (bf16[64,2560]{1,0:T(8,128)(2,1)S(1)}, bf16[64,2560]{1,0:T(8,128)(2,1)S(1)}, u32[]{:S(2)}, u32[]{:S(2)}) collective-permute-start(bf16[64,2560]{1,0:T(8,128)(2,1)S(1)} %collective-permute-done.2.refs_3_), channel_id=1, source_target_pairs={{0,8},{8,0},{1,9},{9,1},{2,10},{10,2},{3,11},{11,3},{4,12},{12,4},... | collective-permute-start | bytes 983048 | tf_op jit(solution)/shard_map/ppermute | solution.py:564
  28.7 15.5 %collective-permute-start.7 = (bf16[64,2560]{1,0:T(8,128)(2,1)S(1)}, bf16[64,2560]{1,0:T(8,128)(2,1)S(1)}, u32[]{:S(2)}, u32[]{:S(2)}) collective-permute-start(bf16[64,2560]{1,0:T(8,128)(2,1)S(1)} %collective-permute-done.1.refs_2_), channel_id=1, source_target_pairs={{0,8},{8,0},{1,9},{9,1},{2,10},{10,2},{3,11},{11,3},{4,12},{12,4},... | collective-permute-start | bytes 983048 | tf_op jit(solution)/shard_map/ppermute | solution.py:564
  41.3 18.8 %collective-permute-start.10 = (bf16[128,2560]{1,0:T(8,128)(2,1)S(1)}, bf16[128,2560]{1,0:T(8,128)(2,1)S(1)}, u32[]{:S(2)}, u32[]{:S(2)}) collective-permute-start(bf16[128,2560]{1,0:T(8,128)(2,1)S(1)} %collective-permute-done.6.refs_0_.refs_4_), channel_id=1, source_target_pairs={{0,8},{8,0},{1,9},{9,1},{2,10},{10,2},{3,11},{11,3},{4,12},{12,4},... | collective-permute-start | bytes 1966088 | tf_op jit(solution)/shard_map/ppermute | solution.py:564
  44.2 15.9 %collective-permute-start.9 = (bf16[64,2560]{1,0:T(8,128)(2,1)S(1)}, bf16[64,2560]{1,0:T(8,128)(2,1)S(1)}, u32[]{:S(2)}, u32[]{:S(2)}) collective-permute-start(bf16[64,2560]{1,0:T(8,128)(2,1)S(1)} %get-tuple-element.44), channel_id=1, source_target_pairs={{0,4},{1,5},{2,6},{3,7},{4,0},{5,1},{6,2},{7,3},{8,12},{9,13},{10,... | collective-permute-start | bytes 983048 | tf_op jit(solution)/shard_map/ppermute | solution.py:524
  60.9 16.5 %collective-permute-start.11 = (bf16[64,2560]{1,0:T(8,128)(2,1)}, bf16[64,2560]{1,0:T(8,128)(2,1)S(1)}, u32[]{:S(2)}, u32[]{:S(2)}) collective-permute-start(bf16[64,2560]{1,0:T(8,128)(2,1)} %get-tuple-element.45), channel_id=1, source_target_pairs={{0,4},{1,5},{2,6},{3,7},{4,0},{5,1},{6,2},{7,3},{8,12},{9,13},{10,... | collective-permute-start | bytes 983048 | tf_op jit(solution)/shard_map/ppermute | solution.py:524
  70.8 9.5 %collective-permute-start.12 = (bf16[64,2560]{1,0:T(8,128)(2,1)S(1)}, bf16[64,2560]{1,0:T(8,128)(2,1)S(1)}, u32[]{:S(2)}, u32[]{:S(2)}) collective-permute-start(bf16[64,2560]{1,0:T(8,128)(2,1)S(1)} %collective-permute-done.9.refs_1_.refs_5_), channel_id=1, source_target_pairs={{0,8},{8,0},{1,9},{9,1},{2,10},{10,2},{3,11},{11,3},{4,12},{12,4},... | collective-permute-start | bytes 983048 | tf_op jit(solution)/shard_map/ppermute | solution.py:564
  77.4 9.8 %collective-permute-start.13 = (bf16[64,2560]{1,0:T(8,128)(2,1)S(1)}, bf16[64,2560]{1,0:T(8,128)(2,1)S(1)}, u32[]{:S(2)}, u32[]{:S(2)}) collective-permute-start(bf16[64,2560]{1,0:T(8,128)(2,1)S(1)} %collective-permute-done.11.refs_2_.refs_6_), channel_id=1, source_target_pairs={{0,8},{8,0},{1,9},{9,1},{2,10},{10,2},{3,11},{11,3},{4,12},{12,4},... | collective-permute-start | bytes 983048 | tf_op jit(solution)/shard_map/ppermute | solution.py:564
  78.4 20.4 %collective-permute-start.16 = (bf16[2,4,64,512]{3,2,1,0:T(8,128)(2,1)S(1)}, bf16[2,4,64,512]{3,2,1,0:T(8,128)(2,1)S(1)}, u32[]{:S(2)}, u32[]{:S(2)}) collective-permute-start(bf16[2,4,64,512]{3,2,1,0:T(8,128)(2,1)S(1)} %bitcast.44), channel_id=1, source_target_pairs={{0,2},{1,3},{2,4},{3,5},{4,6},{5,7},{6,0},{7,1},{8,10},{9,11},{10,... | collective-permute-start | bytes 1572872 | tf_op jit(solution)/shard_map/ppermute | solution.py:524
  96.7 25.9 %collective-permute-start.17 = (bf16[2,4,64,512]{3,2,1,0:T(8,128)(2,1)S(1)}, bf16[2,4,64,512]{3,2,1,0:T(8,128)(2,1)S(1)}, u32[]{:S(2)}, u32[]{:S(2)}) collective-permute-start(bf16[2,4,64,512]{3,2,1,0:T(8,128)(2,1)S(1)} %bitcast.48), channel_id=1, source_target_pairs={{0,2},{1,3},{2,4},{3,5},{4,6},{5,7},{6,0},{7,1},{8,10},{9,11},{10,... | collective-permute-start | bytes 1572872 | tf_op jit(solution)/shard_map/ppermute | solution.py:524
  98.7 24.5 %collective-permute-start.20 = (bf16[2,4,64,512]{3,2,1,0:T(8,128)(2,1)S(1)}, bf16[2,4,64,512]{3,2,1,0:T(8,128)(2,1)S(1)}, u32[]{:S(2)}, u32[]{:S(2)}) collective-permute-start(bf16[2,4,64,512]{3,2,1,0:T(8,128)(2,1)S(1)} %collective-permute-done.16.refs_6_), channel_id=1, source_target_pairs={{0,2},{1,3},{2,4},{3,5},{4,6},{5,7},{6,0},{7,1},{8,10},{9,11},{10,... | collective-permute-start | bytes 1572872 | tf_op jit(solution)/shard_map/ppermute | solution.py:524
  122.6 16.7 %collective-permute-start.21 = (bf16[2,4,64,512]{3,2,1,0:T(8,128)(2,1)S(1)}, bf16[2,4,64,512]{3,2,1,0:T(8,128)(2,1)S(1)}, u32[]{:S(2)}, u32[]{:S(2)}) collective-permute-start(bf16[2,4,64,512]{3,2,1,0:T(8,128)(2,1)S(1)} %collective-permute-done.17.refs_7_), channel_id=1, source_target_pairs={{0,2},{1,3},{2,4},{3,5},{4,6},{5,7},{6,0},{7,1},{8,10},{9,11},{10,... | collective-permute-start | bytes 1572872 | tf_op jit(solution)/shard_map/ppermute | solution.py:524
  122.7 16.6 %collective-permute-start.14 = (bf16[2,4,64,512]{3,2,1,0:T(8,128)(2,1)S(1)}, bf16[2,4,64,512]{3,2,1,0:T(8,128)(2,1)S(1)}, u32[]{:S(2)}, u32[]{:S(2)}) collective-permute-start(bf16[2,4,64,512]{3,2,1,0:T(8,128)(2,1)S(1)} %bitcast.45), channel_id=1, source_target_pairs={{0,1},{1,0},{2,3},{3,2},{4,5},{5,4},{6,7},{7,6},{8,9},{9,8},{10,11... | collective-permute-start | bytes 1572872 | tf_op jit(solution)/shard_map/ppermute | solution.py:524
  122.7 16.6 %collective-permute-start.18 = (bf16[2,4,64,512]{3,2,1,0:T(8,128)(2,1)S(1)}, bf16[2,4,64,512]{3,2,1,0:T(8,128)(2,1)S(1)}, u32[]{:S(2)}, u32[]{:S(2)}) collective-permute-start(bf16[2,4,64,512]{3,2,1,0:T(8,128)(2,1)S(1)} %collective-permute-done.16.refs_6_), channel_id=1, source_target_pairs={{0,1},{1,0},{2,3},{3,2},{4,5},{5,4},{6,7},{7,6},{8,9},{9,8},{10,11... | collective-permute-start | bytes 1572872 | tf_op jit(solution)/shard_map/ppermute | solution.py:524
  123.2 27.3 %collective-permute-start.22 = (bf16[2,4,64,512]{3,2,1,0:T(8,128)(2,1)S(1)}, bf16[2,4,64,512]{3,2,1,0:T(8,128)(2,1)S(1)}, u32[]{:S(2)}, u32[]{:S(2)}) collective-permute-start(bf16[2,4,64,512]{3,2,1,0:T(8,128)(2,1)S(1)} %collective-permute-done.20.refs_10_), channel_id=1, source_target_pairs={{0,1},{1,0},{2,3},{3,2},{4,5},{5,4},{6,7},{7,6},{8,9},{9,8},{10,11... | collective-permute-start | bytes 1572872 | tf_op jit(solution)/shard_map/ppermute | solution.py:524
  123.3 27.2 %collective-permute-start.24 = (bf16[2,4,64,512]{3,2,1,0:T(8,128)(2,1)S(1)}, bf16[2,4,64,512]{3,2,1,0:T(8,128)(2,1)S(1)}, u32[]{:S(2)}, u32[]{:S(2)}) collective-permute-start(bf16[2,4,64,512]{3,2,1,0:T(8,128)(2,1)S(1)} %collective-permute-done.20.refs_10_), channel_id=1, source_target_pairs={{0,2},{1,3},{2,4},{3,5},{4,6},{5,7},{6,0},{7,1},{8,10},{9,11},{10,... | collective-permute-start | bytes 1572872 | tf_op jit(solution)/shard_map/ppermute | solution.py:524
  139.3 19.4 %collective-permute-start.25 = (bf16[2,4,64,512]{3,2,1,0:T(8,128)(2,1)S(1)}, bf16[2,4,64,512]{3,2,1,0:T(8,128)(2,1)S(1)}, u32[]{:S(2)}, u32[]{:S(2)}) collective-permute-start(bf16[2,4,64,512]{3,2,1,0:T(8,128)(2,1)S(1)} %collective-permute-done.21.refs_11_), channel_id=1, source_target_pairs={{0,2},{1,3},{2,4},{3,5},{4,6},{5,7},{6,0},{7,1},{8,10},{9,11},{10,... | collective-permute-start | bytes 1572872 | tf_op jit(solution)/shard_map/ppermute | solution.py:524
  139.3 19.4 %collective-permute-start.15 = (bf16[2,4,64,512]{3,2,1,0:T(8,128)(2,1)S(1)}, bf16[2,4,64,512]{3,2,1,0:T(8,128)(2,1)S(1)}, u32[]{:S(2)}, u32[]{:S(2)}) collective-permute-start(bf16[2,4,64,512]{3,2,1,0:T(8,128)(2,1)S(1)} %bitcast.49), channel_id=1, source_target_pairs={{0,1},{1,0},{2,3},{3,2},{4,5},{5,4},{6,7},{7,6},{8,9},{9,8},{10,11... | collective-permute-start | bytes 1572872 | tf_op jit(solution)/shard_map/ppermute | solution.py:524
  139.3 19.4 %collective-permute-start.19 = (bf16[2,4,64,512]{3,2,1,0:T(8,128)(2,1)S(1)}, bf16[2,4,64,512]{3,2,1,0:T(8,128)(2,1)S(1)}, u32[]{:S(2)}, u32[]{:S(2)}) collective-permute-start(bf16[2,4,64,512]{3,2,1,0:T(8,128)(2,1)S(1)} %collective-permute-done.17.refs_7_), channel_id=1, source_target_pairs={{0,1},{1,0},{2,3},{3,2},{4,5},{5,4},{6,7},{7,6},{8,9},{9,8},{10,11... | collective-permute-start | bytes 1572872 | tf_op jit(solution)/shard_map/ppermute | solution.py:524
  150.5 8.1 %collective-permute-start.26 = (bf16[2,4,64,512]{3,2,1,0:T(8,128)(2,1)S(1)}, bf16[2,4,64,512]{3,2,1,0:T(8,128)(2,1)S(1)}, u32[]{:S(2)}, u32[]{:S(2)}) collective-permute-start(bf16[2,4,64,512]{3,2,1,0:T(8,128)(2,1)S(1)} %collective-permute-done.24.refs_14_), channel_id=1, source_target_pairs={{0,1},{1,0},{2,3},{3,2},{4,5},{5,4},{6,7},{7,6},{8,9},{9,8},{10,11... | collective-permute-start | bytes 1572872 | tf_op jit(solution)/shard_map/ppermute | solution.py:524
  150.5 8.2 %collective-permute-start.23 = (bf16[2,4,64,512]{3,2,1,0:T(8,128)(2,1)S(1)}, bf16[2,4,64,512]{3,2,1,0:T(8,128)(2,1)S(1)}, u32[]{:S(2)}, u32[]{:S(2)}) collective-permute-start(bf16[2,4,64,512]{3,2,1,0:T(8,128)(2,1)S(1)} %collective-permute-done.21.refs_11_), channel_id=1, source_target_pairs={{0,1},{1,0},{2,3},{3,2},{4,5},{5,4},{6,7},{7,6},{8,9},{9,8},{10,11... | collective-permute-start | bytes 1572872 | tf_op jit(solution)/shard_map/ppermute | solution.py:524
  158.7 1.9 collective-permute-start.27
  170.9 14.0 %collective-permute-start.28 = (bf16[4,2,128,256]{3,2,1,0:T(8,128)(2,1)S(1)}, bf16[4,2,128,256]{3,2,1,0:T(8,128)(2,1)S(1)}, u32[]{:S(2)}, u32[]{:S(2)}) collective-permute-start(bf16[4,2,128,256]{3,2,1,0:T(8,128)(2,1)S(1)} %get-tuple-element.60), channel_id=1, source_target_pairs={{0,8},{8,0},{1,9},{9,1},{2,10},{10,2},{3,11},{11,3},{4,12},{12,4},... | collective-permute-start | bytes 1572872 | tf_op jit(solution)/shard_map/ppermute | solution.py:564
  189.7 24.4 %collective-permute-start.29 = (bf16[512,1024]{1,0:T(8,128)(2,1)S(1)}, bf16[512,1024]{1,0:T(8,128)(2,1)S(1)}, u32[]{:S(2)}, u32[]{:S(2)}) collective-permute-start(bf16[512,1024]{1,0:T(8,128)(2,1)S(1)} %send_part.2.refs_3_), channel_id=1, source_target_pairs={{0,8},{8,0},{1,9},{9,1},{2,10},{10,2},{3,11},{11,3},{4,12},{12,4},... | collective-permute-start | bytes 3145736 | tf_op jit(solution)/shard_map/ppermute | solution.py:564
  214.1 25.6 %collective-permute-start.34 = (bf16[512,1024]{1,0:T(8,128)(2,1)S(1)}, bf16[512,1024]{1,0:T(8,128)(2,1)S(1)}, u32[]{:S(2)}, u32[]{:S(2)}) collective-permute-start(bf16[512,1024]{1,0:T(8,128)(2,1)S(1)} %get-tuple-element.70), channel_id=1, source_target_pairs={{0,8},{8,0},{1,9},{9,1},{2,10},{10,2},{3,11},{11,3},{4,12},{12,4},... | collective-permute-start | bytes 3145736 | tf_op jit(solution)/shard_map/ppermute | solution.py:564
  216.7 11.1 %collective-permute-start.30 = (bf16[2,64,1024]{2,1,0:T(8,128)(2,1)S(1)}, bf16[2,64,1024]{2,1,0:T(8,128)(2,1)S(1)}, u32[]{:S(2)}, u32[]{:S(2)}) collective-permute-start(bf16[2,64,1024]{2,1,0:T(8,128)(2,1)S(1)} %get-tuple-element.64), channel_id=1, source_target_pairs={{0,2},{1,3},{2,4},{3,5},{4,6},{5,7},{6,0},{7,1},{8,10},{9,11},{10,... | collective-permute-start | bytes 786440 | tf_op jit(solution)/shard_map/ppermute | solution.py:524
  216.8 13.3 %collective-permute-start.31 = (bf16[2,64,1024]{2,1,0:T(8,128)(2,1)S(1)}, bf16[2,64,1024]{2,1,0:T(8,128)(2,1)S(1)}, u32[]{:S(2)}, u32[]{:S(2)}) collective-permute-start(bf16[2,64,1024]{2,1,0:T(8,128)(2,1)S(1)} %get-tuple-element.65), channel_id=1, source_target_pairs={{0,6},{1,7},{2,0},{3,1},{4,2},{5,3},{6,4},{7,5},{8,14},{9,15},{10,... | collective-permute-start | bytes 786440 | tf_op jit(solution)/shard_map/ppermute | solution.py:524
  220.6 19.1 %collective-permute-start.32 = (bf16[2,64,1024]{2,1,0:T(8,128)(2,1)S(1)}, bf16[2,64,1024]{2,1,0:T(8,128)(2,1)S(1)}, u32[]{:S(2)}, u32[]{:S(2)}) collective-permute-start(bf16[2,64,1024]{2,1,0:T(8,128)(2,1)S(1)} %get-tuple-element.66), channel_id=1, source_target_pairs={{0,4},{1,5},{2,6},{3,7},{4,0},{5,1},{6,2},{7,3},{8,12},{9,13},{10,... | collective-permute-start | bytes 786440 | tf_op jit(solution)/shard_map/ppermute | solution.py:524
  239.7 11.7 %collective-permute-start.39 = (bf16[512,512]{1,0:T(8,128)(2,1)S(1)}, bf16[512,512]{1,0:T(8,128)(2,1)S(1)}, u32[]{:S(2)}, u32[]{:S(2)}) collective-permute-start(bf16[512,512]{1,0:T(8,128)(2,1)S(1)} %get-tuple-element.75.refs_3_), channel_id=1, source_target_pairs={{0,8},{8,0},{1,9},{9,1},{2,10},{10,2},{3,11},{11,3},{4,12},{12,4},... | collective-permute-start | bytes 1572872 | tf_op jit(solution)/shard_map/ppermute | solution.py:564
  241.6 12.3 %collective-permute-start.35 = (bf16[2,64,1024]{2,1,0:T(8,128)(2,1)S(1)}, bf16[2,64,1024]{2,1,0:T(8,128)(2,1)S(1)}, u32[]{:S(2)}, u32[]{:S(2)}) collective-permute-start(bf16[2,64,1024]{2,1,0:T(8,128)(2,1)S(1)} %get-tuple-element.72), channel_id=1, source_target_pairs={{0,2},{1,3},{2,4},{3,5},{4,6},{5,7},{6,0},{7,1},{8,10},{9,11},{10,... | collective-permute-start | bytes 786440 | tf_op jit(solution)/shard_map/ppermute | solution.py:524
  241.7 13.4 %collective-permute-start.36 = (bf16[2,64,1024]{2,1,0:T(8,128)(2,1)S(1)}, bf16[2,64,1024]{2,1,0:T(8,128)(2,1)S(1)}, u32[]{:S(2)}, u32[]{:S(2)}) collective-permute-start(bf16[2,64,1024]{2,1,0:T(8,128)(2,1)S(1)} %get-tuple-element.73), channel_id=1, source_target_pairs={{0,6},{1,7},{2,0},{3,1},{4,2},{5,3},{6,4},{7,5},{8,14},{9,15},{10,... | collective-permute-start | bytes 786440 | tf_op jit(solution)/shard_map/ppermute | solution.py:524
  245.5 22.4 %collective-permute-start.37 = (bf16[2,64,1024]{2,1,0:T(8,128)(2,1)S(1)}, bf16[2,64,1024]{2,1,0:T(8,128)(2,1)S(1)}, u32[]{:S(2)}, u32[]{:S(2)}) collective-permute-start(bf16[2,64,1024]{2,1,0:T(8,128)(2,1)S(1)} %get-tuple-element.74), channel_id=1, source_target_pairs={{0,4},{1,5},{2,6},{3,7},{4,0},{5,1},{6,2},{7,3},{8,12},{9,13},{10,... | collective-permute-start | bytes 786440 | tf_op jit(solution)/shard_map/ppermute | solution.py:524
  252.9 16.6 %collective-permute-start.40 = (bf16[2,64,512]{2,1,0:T(8,128)(2,1)S(1)}, bf16[2,64,512]{2,1,0:T(8,128)(2,1)S(1)}, u32[]{:S(2)}, u32[]{:S(2)}) collective-permute-start(bf16[2,64,512]{2,1,0:T(8,128)(2,1)S(1)} %get-tuple-element.77), channel_id=1, source_target_pairs={{0,2},{1,3},{2,4},{3,5},{4,6},{5,7},{6,0},{7,1},{8,10},{9,11},{10,... | collective-permute-start | bytes 393224 | tf_op jit(solution)/shard_map/ppermute | solution.py:524
  253.8 22.7 %collective-permute-start.33 = (bf16[4,64,1024]{2,1,0:T(8,128)(2,1)}, bf16[4,64,1024]{2,1,0:T(8,128)(2,1)}, u32[]{:S(2)}, u32[]{:S(2)}) collective-permute-start(bf16[4,64,1024]{2,1,0:T(8,128)(2,1)} %pad_maximum_fusion.3), channel_id=1, source_target_pairs={{0,1},{1,0},{2,3},{3,2},{4,5},{5,4},{6,7},{7,6},{8,9},{9,8},{10,11... | collective-permute-start | bytes 1572872 | tf_op jit(solution)/shard_map/ppermute | solution.py:524
  268.7 6.6 %collective-permute-start.41 = (bf16[2,64,512]{2,1,0:T(8,128)(2,1)}, bf16[2,64,512]{2,1,0:T(8,128)(2,1)S(1)}, u32[]{:S(2)}, u32[]{:S(2)}) collective-permute-start(bf16[2,64,512]{2,1,0:T(8,128)(2,1)} %get-tuple-element.78), channel_id=1, source_target_pairs={{0,6},{1,7},{2,0},{3,1},{4,2},{5,3},{6,4},{7,5},{8,14},{9,15},{10,... | collective-permute-start | bytes 393224 | tf_op jit(solution)/shard_map/ppermute | solution.py:524
  268.7 6.6 %collective-permute-start.42 = (bf16[2,64,512]{2,1,0:T(8,128)(2,1)}, bf16[2,64,512]{2,1,0:T(8,128)(2,1)S(1)}, u32[]{:S(2)}, u32[]{:S(2)}) collective-permute-start(bf16[2,64,512]{2,1,0:T(8,128)(2,1)} %get-tuple-element.79), channel_id=1, source_target_pairs={{0,4},{1,5},{2,6},{3,7},{4,0},{5,1},{6,2},{7,3},{8,12},{9,13},{10,... | collective-permute-start | bytes 393224 | tf_op jit(solution)/shard_map/ppermute | solution.py:524
  269.6 7.0 %collective-permute-start.38 = (bf16[4,64,1024]{2,1,0:T(8,128)(2,1)}, bf16[4,64,1024]{2,1,0:T(8,128)(2,1)}, u32[]{:S(2)}, u32[]{:S(2)}) collective-permute-start(bf16[4,64,1024]{2,1,0:T(8,128)(2,1)} %pad_maximum_fusion.4), channel_id=1, source_target_pairs={{0,1},{1,0},{2,3},{3,2},{4,5},{5,4},{6,7},{7,6},{8,9},{9,8},{10,11... | collective-permute-start | bytes 1572872 | tf_op jit(solution)/shard_map/ppermute | solution.py:524
  269.6 14.7 %collective-permute-start.44 = (bf16[4,2,128,256]{3,2,1,0:T(8,128)(2,1)}, bf16[4,2,128,256]{3,2,1,0:T(8,128)(2,1)}, u32[]{:S(2)}, u32[]{:S(2)}) collective-permute-start(bf16[4,2,128,256]{3,2,1,0:T(8,128)(2,1)} %get-tuple-element.81), channel_id=1, source_target_pairs={{0,8},{8,0},{1,9},{9,1},{2,10},{10,2},{3,11},{11,3},{4,12},{12,4},... | collective-permute-start | bytes 1572872 | tf_op jit(solution)/shard_map/ppermute | solution.py:564
  275.3 1.6 collective-permute-start.43
  (31 other events, 366.0 us)
where the time goes:
time: 288 us; the launch traced here: 287 us
  waiting for transfers between devices  142 us (49%)
  Pallas kernels  90.7 us (31%)
  starting transfers between devices  37.3 us (13%)
  local copies, waits for them, and re-layouts  8.24 us (3%)
  other arithmetic  7.35 us (3%)
    ppermute x32, waiting for transfers between devices, shift(): return lax.ppermute(x, 'group', pairs)  114 us
    ppermute x13, waiting for transfers between devices, local(): cross = lambda x: lax.ppermute(x, 'tensor', swap)  27.9 us
    pallas_call x2, Pallas kernels, make_q(): pl.pallas_call(functools.partial(q_kernel, sides), grid_spec=pltpu.Prefet...  22.6 us
    ppermute x32, starting transfers between devices, shift(): return lax.ppermute(x, 'group', pairs)  22.5 us
    pallas_call x2, Pallas kernels, make_attention(): pl.pallas_call(functools.partial(attention_kernel, lay, spans, most, per_...  21.3 us
    pallas_call x3, Pallas kernels, make_projection(): pl.pallas_call(functools.partial(project_kernel, len(attended), len(follo...  20.7 us
    pallas_call x2, Pallas kernels, make_kv(): pl.pallas_call(functools.partial(kv_kernel, sides, blocks), grid_spec=plt...  17.4 us
    ppermute x13, starting transfers between devices, local(): cross = lambda x: lax.ppermute(x, 'tensor', swap)  14.9 us
  transfers between devices with their start and end apart: 45, of which 23 were waited for; matrix products, arithmetic and copies ran while one was open for 2% of the time, Pallas kernels for 26%

commit v1 on v0

--- a/solution.py
+++ b/solution.py
@@ -681,15 +681,18 @@
                 for hop, x in zip(hop_order(chips), moved)
             ]
             landed.append(same)
-            swapped = shift(jnp.concatenate([x[1:] for x in same]), owners, 0, 1)
-            pieces.append((same, swapped))
+            pieces.append(same)
             first += sent.shape[1]
-        mixed = make_placed(lay, table, pieces, cols).reshape(1, span_len, cols)
-        for cut in pages[1:]:
-            others.append(cross(after(cut, received[-1])))
+        others += [cross(after(cut, moved[0])) for cut in pages[1:]]
         low = [jnp.where(tensor_rank == 0, a, b) for a, b in zip(pages, others)]
         high = [jnp.where(tensor_rank == 0, b, a) for a, b in zip(pages, others)]
         cache = jnp.concatenate(low + high, axis=3)
+        for n, same in enumerate(pieces):
+            flipped = jnp.concatenate([x[1:] for x in same])
+            if n == len(pieces) - 2:
+                flipped = after(flipped, others)
+            pieces[n] = (same, shift(flipped, owners, 0, 1))
+        mixed = make_placed(lay, after(table, cache), pieces, cols).reshape(1, span_len, cols)
     else:
         pages = jnp.concatenate(pages, axis=3)
         attended = jnp.concatenate(attended, axis=1)

time: 288 us -> 286 us (level)
  starting transfers between devices: 37.3 us -> 43.9 us
  waiting for transfers between devices: 142 us -> 136 us
  other arithmetic: 7.35 us -> 3.5 us
  local copies, waits for them, and re-layouts: 8.24 us -> 11.9 us
    ppermute x32, starting transfers between devices: 22.5 us -> 29.2 us  [shift(): return lax.ppermute(x, 'group', pairs)]
    ppermute x13, waiting for transfers between devices: 27.9 us -> 21.7 us  [local(): cross = lambda x: lax.ppermute(x, 'tensor', swap)]
    unnamed x62 -> x60, local copies, waits for them, and re-layouts: 4.55 us -> 8.27 us
  transfers between devices with their start and end apart: 45 -> 45, of which waited for: 23 -> 21; matrix products, arithmetic and copies ran while one was open for 2% -> 2% of each run, Pallas kernels for 26% -> 25%
where the time goes in v1:
time: 286 us; the launch traced here: 285 us
  waiting for transfers between devices  136 us (48%)
  Pallas kernels  89 us (31%)
  starting transfers between devices  43.9 us (15%)
  local copies, waits for them, and re-layouts  11.9 us (4%)
  other arithmetic  3.5 us (1%)
    ppermute x32, waiting for transfers between devices, shift(): return lax.ppermute(x, 'group', pairs)  114 us
    ppermute x32, starting transfers between devices, shift(): return lax.ppermute(x, 'group', pairs)  29.2 us
    pallas_call x2, Pallas kernels, make_q(): pl.pallas_call(functools.partial(q_kernel, sides), grid_spec=pltpu.Prefet...  22.6 us
    ppermute x13, waiting for transfers between devices, local(): cross = lambda x: lax.ppermute(x, 'tensor', swap)  21.7 us
    pallas_call x3, Pallas kernels, make_projection(): pl.pallas_call(functools.partial(project_kernel, len(attended), len(follo...  21.4 us
    pallas_call x2, Pallas kernels, make_attention(): pl.pallas_call(functools.partial(attention_kernel, lay, spans, most, per_...  19.8 us
    pallas_call x2, Pallas kernels, make_kv(): pl.pallas_call(functools.partial(kv_kernel, sides, blocks), grid_spec=plt...  17.4 us
    ppermute x13, starting transfers between devices, local(): cross = lambda x: lax.ppermute(x, 'tensor', swap)  14.7 us
  transfers between devices with their start and end apart: 45, of which 21 were waited for; matrix products, arithmetic and copies ran while one was open for 2% of the time, Pallas kernels for 25%

profile of v1, /device:TPU:0, one launch (start us, length us, event | category | flops | bytes accessed | tf_op | source)
XLA Modules:
  0.0 285.4 jit_solution(2640581259386872069)
XLA Ops:
  0.7 2.6 dynamic-slice_bitcast_fusion
  4.0 2.7 collective-permute-start.2
  6.7 1.6 collective-permute-start.1
  8.3 1.5 collective-permute-start.3
  11.2 1.5 collective-permute-start.4
  12.7 4.0 %collective-permute-done.2.refs_3_ = bf16[64,2560]{1,0:T(8,128)(2,1)S(1)} collective-permute-done((bf16[64,2560]{1,0:T(8,128)(2,1)S(1)}, bf16[64,2560]{1,0:T(8,128)(2,1)S(1)}, u32[]{:S(2)}, u32[]{:S(2)}) %collective-permute-start.2) | collective-permute-done | bytes 327712 | tf_op jit(solution)/shard_map/ppermute | solution.py:524
  16.7 7.3 %collective-permute-done.1.refs_2_ = bf16[64,2560]{1,0:T(8,128)(2,1)S(1)} collective-permute-done((bf16[64,2560]{1,0:T(8,128)(2,1)S(1)}, bf16[64,2560]{1,0:T(8,128)(2,1)S(1)}, u32[]{:S(2)}, u32[]{:S(2)}) %collective-permute-start.1) | collective-permute-done | bytes 327712 | tf_op jit(solution)/shard_map/ppermute | solution.py:524
  25.6 2.2 collective-permute-start.8
  27.9 1.5 collective-permute-start.6
  29.9 12.0 %collective-permute-done.8.refs_0_.refs_4_ = bf16[128,2560]{1,0:T(8,128)(2,1)S(1)} collective-permute-done((bf16[128,2560]{1,0:T(8,128)(2,1)S(1)}, bf16[128,2560]{1,0:T(8,128)(2,1)S(1)}, u32[]{:S(2)}, u32[]{:S(2)}) %collective-permute-start.8) | collective-permute-done | bytes 655392 | tf_op jit(solution)/shard_map/ppermute | solution.py:524
  42.0 1.3 collective-permute-start.10
  43.4 1.4 tables.1.table
  47.4 14.9 %collective-permute-done.9.refs_1_.refs_5_ = bf16[64,2560]{1,0:T(8,128)(2,1)S(1)} collective-permute-done((bf16[64,2560]{1,0:T(8,128)(2,1)}, bf16[64,2560]{1,0:T(8,128)(2,1)S(1)}, u32[]{:S(2)}, u32[]{:S(2)}) %collective-permute-start.9) | collective-permute-done | bytes 327712 | tf_op jit(solution)/shard_map/ppermute | solution.py:524
  64.4 8.7 %keys_values.2 = (bf16[256,2560]{1,0:T(8,128)(2,1)S(1)}, bf16[256,2560]{1,0:T(8,128)(2,1)S(1)}, bf16[2,256,512]{2,1,0:T(8,128)(2,1)S(1)}) custom-call(s32[130]{0:T(256)S(1)} %tables.1.table, bf16[64,2560]{1,0:T(8,128)(2,1)S(1)} %get-tuple-element.93.refs_0_, bf16[64,2560]{1,0:T(8,128)(2,1)S(1)} %get-tuple-element.100.refs_1_, ...), custom_call_target="tpu_custom_call" | custom-call | flops 53687092 | bytes 314572 | tf_op jit(solution)/shard_map/keys_values/pallas_call | solution.py:180
  73.9 5.8 %collective-permute-done.11.refs_2_.refs_6_ = bf16[64,2560]{1,0:T(8,128)(2,1)S(1)} collective-permute-done((bf16[64,2560]{1,0:T(8,128)(2,1)}, bf16[64,2560]{1,0:T(8,128)(2,1)S(1)}, u32[]{:S(2)}, u32[]{:S(2)}) %collective-permute-start.11) | collective-permute-done | bytes 327712 | tf_op jit(solution)/shard_map/ppermute | solution.py:524
  80.6 2.1 collective-permute-done.12.refs_4_
  82.7 6.8 %collective-permute-done.13.refs_5_ = bf16[64,2560]{1,0:T(8,128)(2,1)S(1)} collective-permute-done((bf16[64,2560]{1,0:T(8,128)(2,1)S(1)}, bf16[64,2560]{1,0:T(8,128)(2,1)S(1)}, u32[]{:S(2)}, u32[]{:S(2)}) %collective-permute-start.13) | collective-permute-done | bytes 327712 | tf_op jit(solution)/shard_map/ppermute | solution.py:564
  90.3 8.7 %keys_values.3 = (bf16[256,2560]{1,0:T(8,128)(2,1)S(1)}, bf16[256,2560]{1,0:T(8,128)(2,1)S(1)}, bf16[2,256,512]{2,1,0:T(8,128)(2,1)S(1)}) custom-call(s32[130]{0:T(256)S(1)} %tables.1.table, bf16[128,2560]{1,0:T(8,128)(2,1)S(1)} %collective-permute-done.8.refs_0_.refs_4_, bf16[64,2560]{1,0:T(8,128)(2,1)S(1)} %collective-permute-done.9.refs_1_.refs_5_, ...), custom_call_target="tpu_custom_call" | custom-call | flops 53687092 | bytes 314572 | tf_op jit(solution)/shard_map/keys_values/pallas_call | solution.py:180
  99.0 2.0 collective-permute-start.17
  102.3 11.3 %queries.2 = bf16[256,2048]{1,0:T(8,128)(2,1)S(1)} custom-call(s32[130]{0:T(256)S(1)} %tables.1.table, bf16[256,2560]{1,0:T(8,128)(2,1)S(1)} %get-tuple-element.45.refs_0_, bf16[256,2560]{1,0:T(8,128)(2,1)S(1)} %get-tuple-element.46.refs_1_, bf16[5120,2048]{1,0:T(8,128)(2,1)} %refs_3_.3, bf16[5120,2048]{1,0:T(8,128)(2,1)} %refs_3_.3, ...), custom_call_target="tpu_custom_call" | custom-call | flops 107374184 | bytes 492830 | tf_op jit(solution)/shard_map/queries/pallas_call | solution.py:237
  113.6 11.3 %queries.3 = bf16[256,2048]{1,0:T(8,128)(2,1)S(1)} custom-call(s32[130]{0:T(256)S(1)} %tables.1.table, bf16[256,2560]{1,0:T(8,128)(2,1)S(1)} %get-tuple-element.54.refs_0_, bf16[256,2560]{1,0:T(8,128)(2,1)S(1)} %get-tuple-element.55.refs_1_, bf16[5120,2048]{1,0:T(8,128)(2,1)} %refs_3_.3, bf16[5120,2048]{1,0:T(8,128)(2,1)} %refs_3_.3, ...), custom_call_target="tpu_custom_call" | custom-call | flops 107374184 | bytes 492830 | tf_op jit(solution)/shard_map/queries/pallas_call | solution.py:237
  125.7 1.6 collective-permute-start.24
  127.2 14.4 %collective-permute-done.21.refs_11_ = bf16[2,4,64,512]{3,2,1,0:T(8,128)(2,1)S(1)} collective-permute-done((bf16[2,4,64,512]{3,2,1,0:T(8,128)(2,1)S(1)}, bf16[2,4,64,512]{3,2,1,0:T(8,128)(2,1)S(1)}, u32[]{:S(2)}, u32[]{:S(2)}) %collective-permute-start.21) | collective-permute-done | bytes 524320 | tf_op jit(solution)/shard_map/ppermute | solution.py:524
  142.2 10.7 %collective-permute-done.24.refs_14_ = bf16[2,4,64,512]{3,2,1,0:T(8,128)(2,1)S(1)} collective-permute-done((bf16[2,4,64,512]{3,2,1,0:T(8,128)(2,1)S(1)}, bf16[2,4,64,512]{3,2,1,0:T(8,128)(2,1)S(1)}, u32[]{:S(2)}, u32[]{:S(2)}) %collective-permute-start.24) | collective-permute-done | bytes 524320 | tf_op jit(solution)/shard_map/ppermute | solution.py:524
  153.4 7.7 %collective-permute-done.25.refs_15_ = bf16[2,4,64,512]{3,2,1,0:T(8,128)(2,1)S(1)} collective-permute-done((bf16[2,4,64,512]{3,2,1,0:T(8,128)(2,1)S(1)}, bf16[2,4,64,512]{3,2,1,0:T(8,128)(2,1)S(1)}, u32[]{:S(2)}, u32[]{:S(2)}) %collective-permute-start.25) | collective-permute-done | bytes 524320 | tf_op jit(solution)/shard_map/ppermute | solution.py:524
  161.1 1.9 collective-permute-done.27.refs_17_
  163.0 9.9 %attention.2 = (bf16[8,64,1024]{2,1,0:T(8,128)(2,1)S(1)}, bf16[4,2,128,256]{3,2,1,0:T(8,128)(2,1)S(1)}) custom-call(s32[130]{0:T(256)S(1)} %tables.1.table, bf16[4,64,2048]{2,1,0:T(8,128)(2,1)S(1)} %bitcast.40, bf16[4,64,2048]{2,1,0:T(8,128)(2,1)S(1)} %bitcast.42, bf16[2,4,64,512]{3,2,1,0:T(8,128)(2,1)S(1)} %bitcast.46, ...), custom_call_target="tpu_custom_call" | custom-call | flops 47244640 | bytes 251658 | tf_op jit(solution)/shard_map/attention/pallas_call | solution.py:355
  172.9 1.4 collective-permute-start.28
  174.2 9.9 %attention.3 = (bf16[8,64,1024]{2,1,0:T(8,128)(2,1)S(1)}, bf16[4,2,128,256]{3,2,1,0:T(8,128)(2,1)S(1)}) custom-call(s32[130]{0:T(256)S(1)} %tables.1.table, bf16[4,64,2048]{2,1,0:T(8,128)(2,1)S(1)} %bitcast.41, bf16[4,64,2048]{2,1,0:T(8,128)(2,1)S(1)} %bitcast.43, bf16[2,4,64,512]{3,2,1,0:T(8,128)(2,1)S(1)} %bitcast.47, ...), custom_call_target="tpu_custom_call" | custom-call | flops 47244640 | bytes 251658 | tf_op jit(solution)/shard_map/attention/pallas_call | solution.py:355
  184.2 2.8 collective-permute-done.28.refs_3_
  186.9 4.8 %send_part.2.refs_3_ = bf16[512,1024]{1,0:T(8,128)(2,1)S(1)} custom-call(s32[130]{0:T(256)S(1)} %tables.1.table, bf16[512,1024]{1,0:T(8,128)(2,1)S(1)} %bitcast.34, bf16[512,1024]{1,0:T(8,128)(2,1)S(1)} %bitcast.37, bf16[2048,5120]{1,0:T(8,128)(2,1)} %refs_2_.9, bf16[4,2,128,256]{3,2,1,0:T(8,128)(2,1)S(1)} %collective-permute-done.28.refs_3_), custom_call_target="tpu_custom_call" | custom-call | flops 42949672 | bytes 146800 | tf_op jit(solution)/shard_map/send_part/pallas_call | solution.py:406
  191.7 1.4 collective-permute-start.29
  193.1 7.2 %send_part.3 = (bf16[512,1024]{1,0:T(8,128)(2,1)S(1)}, bf16[512,512]{1,0:T(8,128)(2,1)}) custom-call(s32[130]{0:T(256)S(1)} %tables.1.table, bf16[512,1024]{1,0:T(8,128)(2,1)S(1)} %bitcast.35, bf16[512,1024]{1,0:T(8,128)(2,1)S(1)} %bitcast.38, bf16[2048,5120]{1,0:T(8,128)(2,1)} %refs_2_.9, bf16[512,1024]{1,0:T(8,128)(2,1)S(1)} %send_part.2.refs_3_), custom_call_target="tpu_custom_call" | custom-call | flops 64424508 | bytes 199229 | tf_op jit(solution)/shard_map/send_part/pallas_call | solution.py:406
  200.2 9.5 %own_part.1 = (bf16[512,1024]{1,0:T(8,128)(2,1)S(1)}, bf16[512,1024]{1,0:T(8,128)(2,1)S(1)}, bf16[512,512]{1,0:T(8,128)(2,1)S(1)}) custom-call(s32[130]{0:T(256)S(1)} %tables.1.table, bf16[512,1024]{1,0:T(8,128)(2,1)S(1)} %bitcast.36, bf16[512,1024]{1,0:T(8,128)(2,1)S(1)} %bitcast.39, bf16[2048,5120]{1,0:T(8,128)(2,1)} %refs_2_.9, ...), custom_call_target="tpu_custom_call" | custom-call | flops 107374184 | bytes 304087 | tf_op jit(solution)/shard_map/own_part/pallas_call | solution.py:406
  210.7 5.4 %collective-permute-done.29 = bf16[512,1024]{1,0:T(8,128)(2,1)S(1)} collective-permute-done((bf16[512,1024]{1,0:T(8,128)(2,1)S(1)}, bf16[512,1024]{1,0:T(8,128)(2,1)S(1)}, u32[]{:S(2)}, u32[]{:S(2)}) %collective-permute-start.29) | collective-permute-done | bytes 1048608 | tf_op jit(solution)/shard_map/ppermute | solution.py:564
  218.6 3.8 %collective-permute-start.32 = (bf16[2,64,1024]{2,1,0:T(8,128)(2,1)S(1)}, bf16[2,64,1024]{2,1,0:T(8,128)(2,1)S(1)}, u32[]{:S(2)}, u32[]{:S(2)}) collective-permute-start(bf16[2,64,1024]{2,1,0:T(8,128)(2,1)S(1)} %get-tuple-element.72), channel_id=1, source_target_pairs={{0,6},{1,7},{2,0},{3,1},{4,2},{5,3},{6,4},{7,5},{8,14},{9,15},{10,... | collective-permute-start | bytes 786440 | tf_op jit(solution)/shard_map/ppermute | solution.py:524
  222.5 7.2 %collective-permute-done.31.refs_1_ = bf16[2,64,1024]{2,1,0:T(8,128)(2,1)S(1)} collective-permute-done((bf16[2,64,1024]{2,1,0:T(8,128)(2,1)S(1)}, bf16[2,64,1024]{2,1,0:T(8,128)(2,1)S(1)}, u32[]{:S(2)}, u32[]{:S(2)}) %collective-permute-start.31) | collective-permute-done | bytes 262176 | tf_op jit(solution)/shard_map/ppermute | solution.py:524
  229.7 2.2 collective-permute-done.32.refs_2_
  231.9 9.7 %collective-permute-done.33.refs_3_ = bf16[2,64,1024]{2,1,0:T(8,128)(2,1)S(1)} collective-permute-done((bf16[2,64,1024]{2,1,0:T(8,128)(2,1)S(1)}, bf16[2,64,1024]{2,1,0:T(8,128)(2,1)S(1)}, u32[]{:S(2)}, u32[]{:S(2)}) %collective-permute-start.33) | collective-permute-done | bytes 262176 | tf_op jit(solution)/shard_map/ppermute | solution.py:524
  247.2 3.8 %collective-permute-start.38 = (bf16[2,64,1024]{2,1,0:T(8,128)(2,1)S(1)}, bf16[2,64,1024]{2,1,0:T(8,128)(2,1)S(1)}, u32[]{:S(2)}, u32[]{:S(2)}) collective-permute-start(bf16[2,64,1024]{2,1,0:T(8,128)(2,1)S(1)} %get-tuple-element.80), channel_id=1, source_target_pairs={{0,6},{1,7},{2,0},{3,1},{4,2},{5,3},{6,4},{7,5},{8,14},{9,15},{10,... | collective-permute-start | bytes 786440 | tf_op jit(solution)/shard_map/ppermute | solution.py:524
  251.1 3.7 %collective-permute-done.34 = bf16[512,512]{1,0:T(8,128)(2,1)} collective-permute-done((bf16[512,512]{1,0:T(8,128)(2,1)}, bf16[512,512]{1,0:T(8,128)(2,1)}, u32[]{:S(2)}, u32[]{:S(2)}) %collective-permute-start.34) | collective-permute-done | bytes 524320 | tf_op jit(solution)/shard_map/ppermute | solution.py:564
  254.8 1.9 residual.4
  258.3 4.6 %collective-permute-start.42 = (bf16[2,64,512]{2,1,0:T(8,128)(2,1)S(1)}, bf16[2,64,512]{2,1,0:T(8,128)(2,1)S(1)}, u32[]{:S(2)}, u32[]{:S(2)}) collective-permute-start(bf16[2,64,512]{2,1,0:T(8,128)(2,1)S(1)} %get-tuple-element.84), channel_id=1, source_target_pairs={{0,6},{1,7},{2,0},{3,1},{4,2},{5,3},{6,4},{7,5},{8,14},{9,15},{10,... | collective-permute-start | bytes 393224 | tf_op jit(solution)/shard_map/ppermute | solution.py:524
  262.9 1.6 collective-permute-start.43
  264.6 13.0 %collective-permute-done.39.refs_8_ = bf16[2,64,1024]{2,1,0:T(8,128)(2,1)S(1)} collective-permute-done((bf16[2,64,1024]{2,1,0:T(8,128)(2,1)S(1)}, bf16[2,64,1024]{2,1,0:T(8,128)(2,1)S(1)}, u32[]{:S(2)}, u32[]{:S(2)}) %collective-permute-start.39) | collective-permute-done | bytes 262176 | tf_op jit(solution)/shard_map/ppermute | solution.py:524
  277.9 2.9 %collective-permute-done.43.refs_13_ = bf16[2,64,512]{2,1,0:T(8,128)(2,1)S(1)} collective-permute-done((bf16[2,64,512]{2,1,0:T(8,128)(2,1)S(1)}, bf16[2,64,512]{2,1,0:T(8,128)(2,1)S(1)}, u32[]{:S(2)}, u32[]{:S(2)}) %collective-permute-start.43) | collective-permute-done | bytes 131104 | tf_op jit(solution)/shard_map/ppermute | solution.py:524
  281.5 1.6 pad_maximum_fusion
  283.2 2.2 placed.1
  (149 shorter events, 26.2 us)
Async XLA Ops:
  3.4 40.0 %copy-start.19 = (s32[8]{0:T(128)S(1)}, s32[8]{0:T(128)}, u32[]{:S(2)}) copy-start(s32[8]{0:T(128)} %source.1) | copy-start | bytes 100
  3.4 40.0 %copy-start.20 = (s32[8]{0:T(128)S(1)}, s32[8]{0:T(128)}, u32[]{:S(2)}) copy-start(s32[8]{0:T(128)} %target.1) | copy-start | bytes 100
  3.5 6.3 %collective-permute-start = (bf16[3,64,2560]{2,1,0:T(8,128)(2,1)S(1)}, bf16[3,64,2560]{2,1,0:T(8,128)(2,1)S(1)}, u32[]{:S(2)}, u32[]{:S(2)}) collective-permute-start(bf16[3,64,2560]{2,1,0:T(8,128)(2,1)S(1)} %pad_maximum_fusion.1), channel_id=1, source_target_pairs={{0,1},{1,0},{2,3},{3,2},{4,5},{5,4},{6,7},{7,6},{8,9},{9,8},{10,11... | collective-permute-start | bytes 2949128 | tf_op jit(solution)/shard_map/ppermute | solution.py:524
  4.0 12.7 %collective-permute-start.2 = (bf16[64,2560]{1,0:T(8,128)(2,1)S(1)}, bf16[64,2560]{1,0:T(8,128)(2,1)S(1)}, u32[]{:S(2)}, u32[]{:S(2)}) collective-permute-start(bf16[64,2560]{1,0:T(8,128)(2,1)S(1)} %get-tuple-element.88), channel_id=1, source_target_pairs={{0,3},{1,2},{2,5},{3,4},{4,7},{5,6},{6,1},{7,0},{8,11},{9,10},{10,... | collective-permute-start | bytes 983048 | tf_op jit(solution)/shard_map/ppermute | solution.py:524
  6.7 17.3 %collective-permute-start.1 = (bf16[64,2560]{1,0:T(8,128)(2,1)S(1)}, bf16[64,2560]{1,0:T(8,128)(2,1)S(1)}, u32[]{:S(2)}, u32[]{:S(2)}) collective-permute-start(bf16[64,2560]{1,0:T(8,128)(2,1)S(1)} %get-tuple-element.89), channel_id=1, source_target_pairs={{0,2},{1,3},{2,4},{3,5},{4,6},{5,7},{6,0},{7,1},{8,10},{9,11},{10,... | collective-permute-start | bytes 983048 | tf_op jit(solution)/shard_map/ppermute | solution.py:524
  8.3 15.7 %collective-permute-start.3 = (bf16[64,2560]{1,0:T(8,128)(2,1)S(1)}, bf16[64,2560]{1,0:T(8,128)(2,1)S(1)}, u32[]{:S(2)}, u32[]{:S(2)}) collective-permute-start(bf16[64,2560]{1,0:T(8,128)(2,1)S(1)} %get-tuple-element.93.refs_0_), channel_id=1, source_target_pairs={{0,8},{8,0},{1,9},{9,1},{2,10},{10,2},{3,11},{11,3},{4,12},{12,4},... | collective-permute-start | bytes 983048 | tf_op jit(solution)/shard_map/ppermute | solution.py:564
  9.8 54.6 %copy-start.16 = (bf16[128]{0:T(256)(128)(2,1)S(1)}, bf16[128]{0:T(256)(128)(2,1)}, u32[]{:S(2)}) copy-start(bf16[128]{0:T(256)(128)(2,1)} %param.18) | copy-start | bytes 772
  9.8 14.2 %collective-permute-start.7 = (bf16[1,2560]{1,0:T(2,128)(2,1)S(1)}, bf16[1,2560]{1,0:T(2,128)(2,1)S(1)}, u32[]{:S(2)}, u32[]{:S(2)}) collective-permute-start(bf16[1,2560]{1,0:T(2,128)(2,1)S(1)} %broadcast_in_dim.6.refs_8_.refs_6_), channel_id=1, source_target_pairs={{0,8},{8,0},{1,9},{9,1},{2,10},{10,2},{3,11},{11,3},{4,12},{12,4},... | collective-permute-start | bytes 15368 | tf_op jit(solution)/shard_map/ppermute | solution.py:564
  11.2 13.7 %collective-permute-start.4 = (bf16[64,2560]{1,0:T(8,128)(2,1)S(1)}, bf16[64,2560]{1,0:T(8,128)(2,1)S(1)}, u32[]{:S(2)}, u32[]{:S(2)}) collective-permute-start(bf16[64,2560]{1,0:T(8,128)(2,1)S(1)} %get-tuple-element.100.refs_1_), channel_id=1, source_target_pairs={{0,8},{8,0},{1,9},{9,1},{2,10},{10,2},{3,11},{11,3},{4,12},{12,4},... | collective-permute-start | bytes 983048 | tf_op jit(solution)/shard_map/ppermute | solution.py:564
  25.6 16.3 %collective-permute-start.8 = (bf16[128,2560]{1,0:T(8,128)(2,1)S(1)}, bf16[128,2560]{1,0:T(8,128)(2,1)S(1)}, u32[]{:S(2)}, u32[]{:S(2)}) collective-permute-start(bf16[128,2560]{1,0:T(8,128)(2,1)S(1)} %pad_maximum_fusion.2), channel_id=1, source_target_pairs={{0,6},{1,7},{2,0},{3,1},{4,2},{5,3},{6,4},{7,5},{8,14},{9,15},{10,... | collective-permute-start | bytes 1966088 | tf_op jit(solution)/shard_map/ppermute | solution.py:524
  27.9 17.0 %collective-permute-start.6 = (bf16[64,2560]{1,0:T(8,128)(2,1)S(1)}, bf16[64,2560]{1,0:T(8,128)(2,1)S(1)}, u32[]{:S(2)}, u32[]{:S(2)}) collective-permute-start(bf16[64,2560]{1,0:T(8,128)(2,1)S(1)} %collective-permute-done.2.refs_3_), channel_id=1, source_target_pairs={{0,8},{8,0},{1,9},{9,1},{2,10},{10,2},{3,11},{11,3},{4,12},{12,4},... | collective-permute-start | bytes 983048 | tf_op jit(solution)/shard_map/ppermute | solution.py:564
  29.4 15.5 %collective-permute-start.5 = (bf16[64,2560]{1,0:T(8,128)(2,1)S(1)}, bf16[64,2560]{1,0:T(8,128)(2,1)S(1)}, u32[]{:S(2)}, u32[]{:S(2)}) collective-permute-start(bf16[64,2560]{1,0:T(8,128)(2,1)S(1)} %collective-permute-done.1.refs_2_), channel_id=1, source_target_pairs={{0,8},{8,0},{1,9},{9,1},{2,10},{10,2},{3,11},{11,3},{4,12},{12,4},... | collective-permute-start | bytes 983048 | tf_op jit(solution)/shard_map/ppermute | solution.py:564
  42.0 20.4 %collective-permute-start.10 = (bf16[128,2560]{1,0:T(8,128)(2,1)S(1)}, bf16[128,2560]{1,0:T(8,128)(2,1)S(1)}, u32[]{:S(2)}, u32[]{:S(2)}) collective-permute-start(bf16[128,2560]{1,0:T(8,128)(2,1)S(1)} %collective-permute-done.8.refs_0_.refs_4_), channel_id=1, source_target_pairs={{0,8},{8,0},{1,9},{9,1},{2,10},{10,2},{3,11},{11,3},{4,12},{12,4},... | collective-permute-start | bytes 1966088 | tf_op jit(solution)/shard_map/ppermute | solution.py:564
  46.3 16.0 %collective-permute-start.9 = (bf16[64,2560]{1,0:T(8,128)(2,1)}, bf16[64,2560]{1,0:T(8,128)(2,1)S(1)}, u32[]{:S(2)}, u32[]{:S(2)}) collective-permute-start(bf16[64,2560]{1,0:T(8,128)(2,1)} %get-tuple-element.48), channel_id=1, source_target_pairs={{0,4},{1,5},{2,6},{3,7},{4,0},{5,1},{6,2},{7,3},{8,12},{9,13},{10,... | collective-permute-start | bytes 983048 | tf_op jit(solution)/shard_map/ppermute | solution.py:524
  63.2 16.5 %collective-permute-start.11 = (bf16[64,2560]{1,0:T(8,128)(2,1)}, bf16[64,2560]{1,0:T(8,128)(2,1)S(1)}, u32[]{:S(2)}, u32[]{:S(2)}) collective-permute-start(bf16[64,2560]{1,0:T(8,128)(2,1)} %get-tuple-element.49), channel_id=1, source_target_pairs={{0,4},{1,5},{2,6},{3,7},{4,0},{5,1},{6,2},{7,3},{8,12},{9,13},{10,... | collective-permute-start | bytes 983048 | tf_op jit(solution)/shard_map/ppermute | solution.py:524
  73.1 9.6 %collective-permute-start.12 = (bf16[64,2560]{1,0:T(8,128)(2,1)S(1)}, bf16[64,2560]{1,0:T(8,128)(2,1)S(1)}, u32[]{:S(2)}, u32[]{:S(2)}) collective-permute-start(bf16[64,2560]{1,0:T(8,128)(2,1)S(1)} %collective-permute-done.9.refs_1_.refs_5_), channel_id=1, source_target_pairs={{0,8},{8,0},{1,9},{9,1},{2,10},{10,2},{3,11},{11,3},{4,12},{12,4},... | collective-permute-start | bytes 983048 | tf_op jit(solution)/shard_map/ppermute | solution.py:564
  79.7 9.9 %collective-permute-start.13 = (bf16[64,2560]{1,0:T(8,128)(2,1)S(1)}, bf16[64,2560]{1,0:T(8,128)(2,1)S(1)}, u32[]{:S(2)}, u32[]{:S(2)}) collective-permute-start(bf16[64,2560]{1,0:T(8,128)(2,1)S(1)} %collective-permute-done.11.refs_2_.refs_6_), channel_id=1, source_target_pairs={{0,8},{8,0},{1,9},{9,1},{2,10},{10,2},{3,11},{11,3},{4,12},{12,4},... | collective-permute-start | bytes 983048 | tf_op jit(solution)/shard_map/ppermute | solution.py:564
  80.6 20.4 %collective-permute-start.16 = (bf16[2,4,64,512]{3,2,1,0:T(8,128)(2,1)S(1)}, bf16[2,4,64,512]{3,2,1,0:T(8,128)(2,1)S(1)}, u32[]{:S(2)}, u32[]{:S(2)}) collective-permute-start(bf16[2,4,64,512]{3,2,1,0:T(8,128)(2,1)S(1)} %bitcast.44), channel_id=1, source_target_pairs={{0,2},{1,3},{2,4},{3,5},{4,6},{5,7},{6,0},{7,1},{8,10},{9,11},{10,... | collective-permute-start | bytes 1572872 | tf_op jit(solution)/shard_map/ppermute | solution.py:524
  99.0 25.9 %collective-permute-start.17 = (bf16[2,4,64,512]{3,2,1,0:T(8,128)(2,1)S(1)}, bf16[2,4,64,512]{3,2,1,0:T(8,128)(2,1)S(1)}, u32[]{:S(2)}, u32[]{:S(2)}) collective-permute-start(bf16[2,4,64,512]{3,2,1,0:T(8,128)(2,1)S(1)} %bitcast.48), channel_id=1, source_target_pairs={{0,2},{1,3},{2,4},{3,5},{4,6},{5,7},{6,0},{7,1},{8,10},{9,11},{10,... | collective-permute-start | bytes 1572872 | tf_op jit(solution)/shard_map/ppermute | solution.py:524
  101.0 24.6 %collective-permute-start.20 = (bf16[2,4,64,512]{3,2,1,0:T(8,128)(2,1)S(1)}, bf16[2,4,64,512]{3,2,1,0:T(8,128)(2,1)S(1)}, u32[]{:S(2)}, u32[]{:S(2)}) collective-permute-start(bf16[2,4,64,512]{3,2,1,0:T(8,128)(2,1)S(1)} %collective-permute-done.16.refs_6_), channel_id=1, source_target_pairs={{0,2},{1,3},{2,4},{3,5},{4,6},{5,7},{6,0},{7,1},{8,10},{9,11},{10,... | collective-permute-start | bytes 1572872 | tf_op jit(solution)/shard_map/ppermute | solution.py:524
  124.9 16.7 %collective-permute-start.21 = (bf16[2,4,64,512]{3,2,1,0:T(8,128)(2,1)S(1)}, bf16[2,4,64,512]{3,2,1,0:T(8,128)(2,1)S(1)}, u32[]{:S(2)}, u32[]{:S(2)}) collective-permute-start(bf16[2,4,64,512]{3,2,1,0:T(8,128)(2,1)S(1)} %collective-permute-done.17.refs_7_), channel_id=1, source_target_pairs={{0,2},{1,3},{2,4},{3,5},{4,6},{5,7},{6,0},{7,1},{8,10},{9,11},{10,... | collective-permute-start | bytes 1572872 | tf_op jit(solution)/shard_map/ppermute | solution.py:524
  125.1 16.6 %collective-permute-start.14 = (bf16[2,4,64,512]{3,2,1,0:T(8,128)(2,1)S(1)}, bf16[2,4,64,512]{3,2,1,0:T(8,128)(2,1)S(1)}, u32[]{:S(2)}, u32[]{:S(2)}) collective-permute-start(bf16[2,4,64,512]{3,2,1,0:T(8,128)(2,1)S(1)} %bitcast.45), channel_id=1, source_target_pairs={{0,1},{1,0},{2,3},{3,2},{4,5},{5,4},{6,7},{7,6},{8,9},{9,8},{10,11... | collective-permute-start | bytes 1572872 | tf_op jit(solution)/shard_map/ppermute | solution.py:524
  125.1 16.6 %collective-permute-start.18 = (bf16[2,4,64,512]{3,2,1,0:T(8,128)(2,1)S(1)}, bf16[2,4,64,512]{3,2,1,0:T(8,128)(2,1)S(1)}, u32[]{:S(2)}, u32[]{:S(2)}) collective-permute-start(bf16[2,4,64,512]{3,2,1,0:T(8,128)(2,1)S(1)} %collective-permute-done.16.refs_6_), channel_id=1, source_target_pairs={{0,1},{1,0},{2,3},{3,2},{4,5},{5,4},{6,7},{7,6},{8,9},{9,8},{10,11... | collective-permute-start | bytes 1572872 | tf_op jit(solution)/shard_map/ppermute | solution.py:524
  125.6 27.3 %collective-permute-start.22 = (bf16[2,4,64,512]{3,2,1,0:T(8,128)(2,1)S(1)}, bf16[2,4,64,512]{3,2,1,0:T(8,128)(2,1)S(1)}, u32[]{:S(2)}, u32[]{:S(2)}) collective-permute-start(bf16[2,4,64,512]{3,2,1,0:T(8,128)(2,1)S(1)} %collective-permute-done.20.refs_10_), channel_id=1, source_target_pairs={{0,1},{1,0},{2,3},{3,2},{4,5},{5,4},{6,7},{7,6},{8,9},{9,8},{10,11... | collective-permute-start | bytes 1572872 | tf_op jit(solution)/shard_map/ppermute | solution.py:524
  125.7 27.2 %collective-permute-start.24 = (bf16[2,4,64,512]{3,2,1,0:T(8,128)(2,1)S(1)}, bf16[2,4,64,512]{3,2,1,0:T(8,128)(2,1)S(1)}, u32[]{:S(2)}, u32[]{:S(2)}) collective-permute-start(bf16[2,4,64,512]{3,2,1,0:T(8,128)(2,1)S(1)} %collective-permute-done.20.refs_10_), channel_id=1, source_target_pairs={{0,2},{1,3},{2,4},{3,5},{4,6},{5,7},{6,0},{7,1},{8,10},{9,11},{10,... | collective-permute-start | bytes 1572872 | tf_op jit(solution)/shard_map/ppermute | solution.py:524
  141.6 19.5 %collective-permute-start.25 = (bf16[2,4,64,512]{3,2,1,0:T(8,128)(2,1)S(1)}, bf16[2,4,64,512]{3,2,1,0:T(8,128)(2,1)S(1)}, u32[]{:S(2)}, u32[]{:S(2)}) collective-permute-start(bf16[2,4,64,512]{3,2,1,0:T(8,128)(2,1)S(1)} %collective-permute-done.21.refs_11_), channel_id=1, source_target_pairs={{0,2},{1,3},{2,4},{3,5},{4,6},{5,7},{6,0},{7,1},{8,10},{9,11},{10,... | collective-permute-start | bytes 1572872 | tf_op jit(solution)/shard_map/ppermute | solution.py:524
  141.6 19.5 %collective-permute-start.15 = (bf16[2,4,64,512]{3,2,1,0:T(8,128)(2,1)S(1)}, bf16[2,4,64,512]{3,2,1,0:T(8,128)(2,1)S(1)}, u32[]{:S(2)}, u32[]{:S(2)}) collective-permute-start(bf16[2,4,64,512]{3,2,1,0:T(8,128)(2,1)S(1)} %bitcast.49), channel_id=1, source_target_pairs={{0,1},{1,0},{2,3},{3,2},{4,5},{5,4},{6,7},{7,6},{8,9},{9,8},{10,11... | collective-permute-start | bytes 1572872 | tf_op jit(solution)/shard_map/ppermute | solution.py:524
  141.7 19.4 %collective-permute-start.19 = (bf16[2,4,64,512]{3,2,1,0:T(8,128)(2,1)S(1)}, bf16[2,4,64,512]{3,2,1,0:T(8,128)(2,1)S(1)}, u32[]{:S(2)}, u32[]{:S(2)}) collective-permute-start(bf16[2,4,64,512]{3,2,1,0:T(8,128)(2,1)S(1)} %collective-permute-done.17.refs_7_), channel_id=1, source_target_pairs={{0,1},{1,0},{2,3},{3,2},{4,5},{5,4},{6,7},{7,6},{8,9},{9,8},{10,11... | collective-permute-start | bytes 1572872 | tf_op jit(solution)/shard_map/ppermute | solution.py:524
  152.9 8.2 %collective-permute-start.26 = (bf16[2,4,64,512]{3,2,1,0:T(8,128)(2,1)S(1)}, bf16[2,4,64,512]{3,2,1,0:T(8,128)(2,1)S(1)}, u32[]{:S(2)}, u32[]{:S(2)}) collective-permute-start(bf16[2,4,64,512]{3,2,1,0:T(8,128)(2,1)S(1)} %collective-permute-done.24.refs_14_), channel_id=1, source_target_pairs={{0,1},{1,0},{2,3},{3,2},{4,5},{5,4},{6,7},{7,6},{8,9},{9,8},{10,11... | collective-permute-start | bytes 1572872 | tf_op jit(solution)/shard_map/ppermute | solution.py:524
  152.9 8.2 %collective-permute-start.23 = (bf16[2,4,64,512]{3,2,1,0:T(8,128)(2,1)S(1)}, bf16[2,4,64,512]{3,2,1,0:T(8,128)(2,1)S(1)}, u32[]{:S(2)}, u32[]{:S(2)}) collective-permute-start(bf16[2,4,64,512]{3,2,1,0:T(8,128)(2,1)S(1)} %collective-permute-done.21.refs_11_), channel_id=1, source_target_pairs={{0,1},{1,0},{2,3},{3,2},{4,5},{5,4},{6,7},{7,6},{8,9},{9,8},{10,11... | collective-permute-start | bytes 1572872 | tf_op jit(solution)/shard_map/ppermute | solution.py:524
  161.1 1.9 collective-permute-start.27
  172.9 14.0 %collective-permute-start.28 = (bf16[4,2,128,256]{3,2,1,0:T(8,128)(2,1)S(1)}, bf16[4,2,128,256]{3,2,1,0:T(8,128)(2,1)S(1)}, u32[]{:S(2)}, u32[]{:S(2)}) collective-permute-start(bf16[4,2,128,256]{3,2,1,0:T(8,128)(2,1)S(1)} %get-tuple-element.60), channel_id=1, source_target_pairs={{0,8},{8,0},{1,9},{9,1},{2,10},{10,2},{3,11},{11,3},{4,12},{12,4},... | collective-permute-start | bytes 1572872 | tf_op jit(solution)/shard_map/ppermute | solution.py:564
  191.7 24.4 %collective-permute-start.29 = (bf16[512,1024]{1,0:T(8,128)(2,1)S(1)}, bf16[512,1024]{1,0:T(8,128)(2,1)S(1)}, u32[]{:S(2)}, u32[]{:S(2)}) collective-permute-start(bf16[512,1024]{1,0:T(8,128)(2,1)S(1)} %send_part.2.refs_3_), channel_id=1, source_target_pairs={{0,8},{8,0},{1,9},{9,1},{2,10},{10,2},{3,11},{11,3},{4,12},{12,4},... | collective-permute-start | bytes 3145736 | tf_op jit(solution)/shard_map/ppermute | solution.py:564
  216.1 25.4 %collective-permute-start.30 = (bf16[512,1024]{1,0:T(8,128)(2,1)S(1)}, bf16[512,1024]{1,0:T(8,128)(2,1)S(1)}, u32[]{:S(2)}, u32[]{:S(2)}) collective-permute-start(bf16[512,1024]{1,0:T(8,128)(2,1)S(1)} %get-tuple-element.69), channel_id=1, source_target_pairs={{0,8},{8,0},{1,9},{9,1},{2,10},{10,2},{3,11},{11,3},{4,12},{12,4},... | collective-permute-start | bytes 3145736 | tf_op jit(solution)/shard_map/ppermute | solution.py:564
  218.6 11.1 %collective-permute-start.31 = (bf16[2,64,1024]{2,1,0:T(8,128)(2,1)S(1)}, bf16[2,64,1024]{2,1,0:T(8,128)(2,1)S(1)}, u32[]{:S(2)}, u32[]{:S(2)}) collective-permute-start(bf16[2,64,1024]{2,1,0:T(8,128)(2,1)S(1)} %get-tuple-element.71), channel_id=1, source_target_pairs={{0,2},{1,3},{2,4},{3,5},{4,6},{5,7},{6,0},{7,1},{8,10},{9,11},{10,... | collective-permute-start | bytes 786440 | tf_op jit(solution)/shard_map/ppermute | solution.py:524
  218.6 13.3 %collective-permute-start.32 = (bf16[2,64,1024]{2,1,0:T(8,128)(2,1)S(1)}, bf16[2,64,1024]{2,1,0:T(8,128)(2,1)S(1)}, u32[]{:S(2)}, u32[]{:S(2)}) collective-permute-start(bf16[2,64,1024]{2,1,0:T(8,128)(2,1)S(1)} %get-tuple-element.72), channel_id=1, source_target_pairs={{0,6},{1,7},{2,0},{3,1},{4,2},{5,3},{6,4},{7,5},{8,14},{9,15},{10,... | collective-permute-start | bytes 786440 | tf_op jit(solution)/shard_map/ppermute | solution.py:524
  222.5 19.1 %collective-permute-start.33 = (bf16[2,64,1024]{2,1,0:T(8,128)(2,1)S(1)}, bf16[2,64,1024]{2,1,0:T(8,128)(2,1)S(1)}, u32[]{:S(2)}, u32[]{:S(2)}) collective-permute-start(bf16[2,64,1024]{2,1,0:T(8,128)(2,1)S(1)} %get-tuple-element.73), channel_id=1, source_target_pairs={{0,4},{1,5},{2,6},{3,7},{4,0},{5,1},{6,2},{7,3},{8,12},{9,13},{10,... | collective-permute-start | bytes 786440 | tf_op jit(solution)/shard_map/ppermute | solution.py:524
  242.7 12.1 %collective-permute-start.34 = (bf16[512,512]{1,0:T(8,128)(2,1)}, bf16[512,512]{1,0:T(8,128)(2,1)}, u32[]{:S(2)}, u32[]{:S(2)}) collective-permute-start(bf16[512,512]{1,0:T(8,128)(2,1)} %get-tuple-element.74.refs_3_), channel_id=1, source_target_pairs={{0,8},{8,0},{1,9},{9,1},{2,10},{10,2},{3,11},{11,3},{4,12},{12,4},... | collective-permute-start | bytes 1572872 | tf_op jit(solution)/shard_map/ppermute | solution.py:564
  247.2 11.1 %collective-permute-start.37 = (bf16[2,64,1024]{2,1,0:T(8,128)(2,1)S(1)}, bf16[2,64,1024]{2,1,0:T(8,128)(2,1)S(1)}, u32[]{:S(2)}, u32[]{:S(2)}) collective-permute-start(bf16[2,64,1024]{2,1,0:T(8,128)(2,1)S(1)} %get-tuple-element.79), channel_id=1, source_target_pairs={{0,2},{1,3},{2,4},{3,5},{4,6},{5,7},{6,0},{7,1},{8,10},{9,11},{10,... | collective-permute-start | bytes 786440 | tf_op jit(solution)/shard_map/ppermute | solution.py:524
  247.2 15.6 %collective-permute-start.38 = (bf16[2,64,1024]{2,1,0:T(8,128)(2,1)S(1)}, bf16[2,64,1024]{2,1,0:T(8,128)(2,1)S(1)}, u32[]{:S(2)}, u32[]{:S(2)}) collective-permute-start(bf16[2,64,1024]{2,1,0:T(8,128)(2,1)S(1)} %get-tuple-element.80), channel_id=1, source_target_pairs={{0,6},{1,7},{2,0},{3,1},{4,2},{5,3},{6,4},{7,5},{8,14},{9,15},{10,... | collective-permute-start | bytes 786440 | tf_op jit(solution)/shard_map/ppermute | solution.py:524
  251.1 26.6 %collective-permute-start.39 = (bf16[2,64,1024]{2,1,0:T(8,128)(2,1)S(1)}, bf16[2,64,1024]{2,1,0:T(8,128)(2,1)S(1)}, u32[]{:S(2)}, u32[]{:S(2)}) collective-permute-start(bf16[2,64,1024]{2,1,0:T(8,128)(2,1)S(1)} %get-tuple-element.81), channel_id=1, source_target_pairs={{0,4},{1,5},{2,6},{3,7},{4,0},{5,1},{6,2},{7,3},{8,12},{9,13},{10,... | collective-permute-start | bytes 786440 | tf_op jit(solution)/shard_map/ppermute | solution.py:524
  256.6 24.1 %collective-permute-start.35 = (bf16[4,2,128,256]{3,2,1,0:T(8,128)(2,1)S(1)}, bf16[4,2,128,256]{3,2,1,0:T(8,128)(2,1)S(1)}, u32[]{:S(2)}, u32[]{:S(2)}) collective-permute-start(bf16[4,2,128,256]{3,2,1,0:T(8,128)(2,1)S(1)} %copy-done.11), channel_id=1, source_target_pairs={{0,8},{8,0},{1,9},{9,1},{2,10},{10,2},{3,11},{11,3},{4,12},{12,4},... | collective-permute-start | bytes 1572872 | tf_op jit(solution)/shard_map/ppermute | solution.py:564
  257.9 19.9 %collective-permute-start.41 = (bf16[2,64,512]{2,1,0:T(8,128)(2,1)S(1)}, bf16[2,64,512]{2,1,0:T(8,128)(2,1)S(1)}, u32[]{:S(2)}, u32[]{:S(2)}) collective-permute-start(bf16[2,64,512]{2,1,0:T(8,128)(2,1)S(1)} %get-tuple-element.83), channel_id=1, source_target_pairs={{0,2},{1,3},{2,4},{3,5},{4,6},{5,7},{6,0},{7,1},{8,10},{9,11},{10,... | collective-permute-start | bytes 393224 | tf_op jit(solution)/shard_map/ppermute | solution.py:524
  258.3 19.5 %collective-permute-start.42 = (bf16[2,64,512]{2,1,0:T(8,128)(2,1)S(1)}, bf16[2,64,512]{2,1,0:T(8,128)(2,1)S(1)}, u32[]{:S(2)}, u32[]{:S(2)}) collective-permute-start(bf16[2,64,512]{2,1,0:T(8,128)(2,1)S(1)} %get-tuple-element.84), channel_id=1, source_target_pairs={{0,6},{1,7},{2,0},{3,1},{4,2},{5,3},{6,4},{7,5},{8,14},{9,15},{10,... | collective-permute-start | bytes 393224 | tf_op jit(solution)/shard_map/ppermute | solution.py:524
  262.9 17.9 %collective-permute-start.43 = (bf16[2,64,512]{2,1,0:T(8,128)(2,1)S(1)}, bf16[2,64,512]{2,1,0:T(8,128)(2,1)S(1)}, u32[]{:S(2)}, u32[]{:S(2)}) collective-permute-start(bf16[2,64,512]{2,1,0:T(8,128)(2,1)S(1)} %get-tuple-element.85), channel_id=1, source_target_pairs={{0,4},{1,5},{2,6},{3,7},{4,0},{5,1},{6,2},{7,3},{8,12},{9,13},{10,... | collective-permute-start | bytes 393224 | tf_op jit(solution)/shard_map/ppermute | solution.py:524
  277.7 5.4 %collective-permute-start.36 = (bf16[4,64,1024]{2,1,0:T(8,128)(2,1)S(1)}, bf16[4,64,1024]{2,1,0:T(8,128)(2,1)S(1)}, u32[]{:S(2)}, u32[]{:S(2)}) collective-permute-start(bf16[4,64,1024]{2,1,0:T(8,128)(2,1)S(1)} %pad_maximum_fusion.3), channel_id=1, source_target_pairs={{0,1},{1,0},{2,3},{3,2},{4,5},{5,4},{6,7},{7,6},{8,9},{9,8},{10,11... | collective-permute-start | bytes 1572872 | tf_op jit(solution)/shard_map/ppermute | solution.py:524
  280.7 2.4 collective-permute-start.40
  280.9 2.3 collective-permute-start.44
  (30 other events, 264.9 us)

commit v2 on v1

--- a/solution.py
+++ b/solution.py
@@ -457,7 +457,7 @@
         compiler_params=params(12),
         cost_estimate=cost(3 * spans * rows * cols, 8 * spans * rows * cols),
         name="residual",
-    )(table, *arrived, own, received)
+    )(table, *arrived, in_hbm(own), in_hbm(received))
 
 
 def place_kernel(lay, chunks, table, *refs):

time: 286 us -> 288 us (level)
  Pallas kernels: 89 us -> 93.8 us
    pallas_call x3, Pallas kernels: 4.15 us -> 7.43 us  [make_sum(): pl.pallas_call(functools.partial(add_kernel, lay, len(arrived)), grid_spe...]
    unnamed x60 -> x46, local copies, waits for them, and re-layouts: 8.27 us -> 6.71 us
  transfers between devices with their start and end apart: 45 -> 45, of which waited for: 21 -> 20; matrix products, arithmetic and copies ran while one was open for 2% -> 2% of each run, Pallas kernels for 25% -> 26%
where the time goes in v2:
time: 288 us; the launch traced here: 287 us
  waiting for transfers between devices  134 us (47%)
  Pallas kernels  93.8 us (33%)
  starting transfers between devices  41.4 us (14%)
  local copies, waits for them, and re-layouts  13 us (5%)
  other arithmetic  3.5 us (1%)
    ppermute x32, waiting for transfers between devices, shift(): return lax.ppermute(x, 'group', pairs)  113 us
    ppermute x32, starting transfers between devices, shift(): return lax.ppermute(x, 'group', pairs)  26.8 us
    pallas_call x2, Pallas kernels, make_q(): pl.pallas_call(functools.partial(q_kernel, sides), grid_spec=pltpu.Prefet...  22.7 us
    pallas_call x3, Pallas kernels, make_projection(): pl.pallas_call(functools.partial(project_kernel, len(attended), len(follo...  21.5 us
    ppermute x13, waiting for transfers between devices, local(): cross = lambda x: lax.ppermute(x, 'tensor', swap)  20.7 us
    pallas_call x2, Pallas kernels, make_attention(): pl.pallas_call(functools.partial(attention_kernel, lay, spans, most, per_...  20 us
    pallas_call x2, Pallas kernels, make_kv(): pl.pallas_call(functools.partial(kv_kernel, sides, blocks), grid_spec=plt...  17.4 us
    ppermute x13, starting transfers between devices, local(): cross = lambda x: lax.ppermute(x, 'tensor', swap)  14.7 us
  transfers between devices with their start and end apart: 45, of which 20 were waited for; matrix products, arithmetic and copies ran while one was open for 2% of the time, Pallas kernels for 26%

profile of v2, /device:TPU:0, one launch (start us, length us, event | category | flops | bytes accessed | tf_op | source)
XLA Modules:
  0.0 287.1 jit_solution(10029204686769247924)
XLA Ops:
  0.7 2.6 dynamic-slice_bitcast_fusion
  4.0 2.7 collective-permute-start.2
  6.7 1.6 collective-permute-start.1
  8.3 1.5 collective-permute-start.3
  11.2 1.5 collective-permute-start.4
  12.7 4.0 %collective-permute-done.2.refs_3_ = bf16[64,2560]{1,0:T(8,128)(2,1)S(1)} collective-permute-done((bf16[64,2560]{1,0:T(8,128)(2,1)S(1)}, bf16[64,2560]{1,0:T(8,128)(2,1)S(1)}, u32[]{:S(2)}, u32[]{:S(2)}) %collective-permute-start.2) | collective-permute-done | bytes 327712 | tf_op jit(solution)/shard_map/ppermute | solution.py:524
  16.7 7.3 %collective-permute-done.1.refs_2_ = bf16[64,2560]{1,0:T(8,128)(2,1)S(1)} collective-permute-done((bf16[64,2560]{1,0:T(8,128)(2,1)S(1)}, bf16[64,2560]{1,0:T(8,128)(2,1)S(1)}, u32[]{:S(2)}, u32[]{:S(2)}) %collective-permute-start.1) | collective-permute-done | bytes 327712 | tf_op jit(solution)/shard_map/ppermute | solution.py:524
  25.6 2.2 collective-permute-start.8
  27.9 1.5 collective-permute-start.6
  29.9 12.0 %collective-permute-done.8.refs_0_.refs_4_ = bf16[128,2560]{1,0:T(8,128)(2,1)S(1)} collective-permute-done((bf16[128,2560]{1,0:T(8,128)(2,1)S(1)}, bf16[128,2560]{1,0:T(8,128)(2,1)S(1)}, u32[]{:S(2)}, u32[]{:S(2)}) %collective-permute-start.8) | collective-permute-done | bytes 655392 | tf_op jit(solution)/shard_map/ppermute | solution.py:524
  43.4 1.4 tables.1.table
  47.4 14.9 %collective-permute-done.9.refs_1_.refs_5_ = bf16[64,2560]{1,0:T(8,128)(2,1)S(1)} collective-permute-done((bf16[64,2560]{1,0:T(8,128)(2,1)}, bf16[64,2560]{1,0:T(8,128)(2,1)S(1)}, u32[]{:S(2)}, u32[]{:S(2)}) %collective-permute-start.9) | collective-permute-done | bytes 327712 | tf_op jit(solution)/shard_map/ppermute | solution.py:524
  63.6 8.7 %keys_values.2 = (bf16[256,2560]{1,0:T(8,128)(2,1)S(1)}, bf16[256,2560]{1,0:T(8,128)(2,1)S(1)}, bf16[2,256,512]{2,1,0:T(8,128)(2,1)S(1)}) custom-call(s32[130]{0:T(256)S(1)} %tables.1.table, bf16[64,2560]{1,0:T(8,128)(2,1)S(1)} %get-tuple-element.93.refs_0_, bf16[64,2560]{1,0:T(8,128)(2,1)S(1)} %get-tuple-element.100.refs_1_, ...), custom_call_target="tpu_custom_call" | custom-call | flops 53687092 | bytes 314572 | tf_op jit(solution)/shard_map/keys_values/pallas_call | solution.py:180
  73.1 5.7 %collective-permute-done.11.refs_2_.refs_6_ = bf16[64,2560]{1,0:T(8,128)(2,1)S(1)} collective-permute-done((bf16[64,2560]{1,0:T(8,128)(2,1)}, bf16[64,2560]{1,0:T(8,128)(2,1)S(1)}, u32[]{:S(2)}, u32[]{:S(2)}) %collective-permute-start.11) | collective-permute-done | bytes 327712 | tf_op jit(solution)/shard_map/ppermute | solution.py:524
  79.8 2.2 collective-permute-done.12.refs_4_
  82.0 6.8 %collective-permute-done.13.refs_5_ = bf16[64,2560]{1,0:T(8,128)(2,1)S(1)} collective-permute-done((bf16[64,2560]{1,0:T(8,128)(2,1)S(1)}, bf16[64,2560]{1,0:T(8,128)(2,1)S(1)}, u32[]{:S(2)}, u32[]{:S(2)}) %collective-permute-start.13) | collective-permute-done | bytes 327712 | tf_op jit(solution)/shard_map/ppermute | solution.py:564
  89.5 8.7 %keys_values.3 = (bf16[256,2560]{1,0:T(8,128)(2,1)S(1)}, bf16[256,2560]{1,0:T(8,128)(2,1)S(1)}, bf16[2,256,512]{2,1,0:T(8,128)(2,1)S(1)}) custom-call(s32[130]{0:T(256)S(1)} %tables.1.table, bf16[128,2560]{1,0:T(8,128)(2,1)S(1)} %collective-permute-done.8.refs_0_.refs_4_, bf16[64,2560]{1,0:T(8,128)(2,1)S(1)} %collective-permute-done.9.refs_1_.refs_5_, ...), custom_call_target="tpu_custom_call" | custom-call | flops 53687092 | bytes 314572 | tf_op jit(solution)/shard_map/keys_values/pallas_call | solution.py:180
  98.2 2.0 collective-permute-start.17
  101.5 11.3 %queries.2 = bf16[256,2048]{1,0:T(8,128)(2,1)S(1)} custom-call(s32[130]{0:T(256)S(1)} %tables.1.table, bf16[256,2560]{1,0:T(8,128)(2,1)S(1)} %get-tuple-element.45.refs_0_, bf16[256,2560]{1,0:T(8,128)(2,1)S(1)} %get-tuple-element.46.refs_1_, bf16[5120,2048]{1,0:T(8,128)(2,1)} %refs_3_.3, bf16[5120,2048]{1,0:T(8,128)(2,1)} %refs_3_.3, ...), custom_call_target="tpu_custom_call" | custom-call | flops 107374184 | bytes 492830 | tf_op jit(solution)/shard_map/queries/pallas_call | solution.py:237
  112.8 11.3 %queries.3 = bf16[256,2048]{1,0:T(8,128)(2,1)S(1)} custom-call(s32[130]{0:T(256)S(1)} %tables.1.table, bf16[256,2560]{1,0:T(8,128)(2,1)S(1)} %get-tuple-element.54.refs_0_, bf16[256,2560]{1,0:T(8,128)(2,1)S(1)} %get-tuple-element.55.refs_1_, bf16[5120,2048]{1,0:T(8,128)(2,1)} %refs_3_.3, bf16[5120,2048]{1,0:T(8,128)(2,1)} %refs_3_.3, ...), custom_call_target="tpu_custom_call" | custom-call | flops 107374184 | bytes 492830 | tf_op jit(solution)/shard_map/queries/pallas_call | solution.py:237
  124.9 1.6 collective-permute-start.24
  126.5 14.4 %collective-permute-done.21.refs_11_ = bf16[2,4,64,512]{3,2,1,0:T(8,128)(2,1)S(1)} collective-permute-done((bf16[2,4,64,512]{3,2,1,0:T(8,128)(2,1)S(1)}, bf16[2,4,64,512]{3,2,1,0:T(8,128)(2,1)S(1)}, u32[]{:S(2)}, u32[]{:S(2)}) %collective-permute-start.21) | collective-permute-done | bytes 524320 | tf_op jit(solution)/shard_map/ppermute | solution.py:524
  141.4 10.7 %collective-permute-done.24.refs_14_ = bf16[2,4,64,512]{3,2,1,0:T(8,128)(2,1)S(1)} collective-permute-done((bf16[2,4,64,512]{3,2,1,0:T(8,128)(2,1)S(1)}, bf16[2,4,64,512]{3,2,1,0:T(8,128)(2,1)S(1)}, u32[]{:S(2)}, u32[]{:S(2)}) %collective-permute-start.24) | collective-permute-done | bytes 524320 | tf_op jit(solution)/shard_map/ppermute | solution.py:524
  152.7 7.7 %collective-permute-done.25.refs_15_ = bf16[2,4,64,512]{3,2,1,0:T(8,128)(2,1)S(1)} collective-permute-done((bf16[2,4,64,512]{3,2,1,0:T(8,128)(2,1)S(1)}, bf16[2,4,64,512]{3,2,1,0:T(8,128)(2,1)S(1)}, u32[]{:S(2)}, u32[]{:S(2)}) %collective-permute-start.25) | collective-permute-done | bytes 524320 | tf_op jit(solution)/shard_map/ppermute | solution.py:524
  160.4 1.9 collective-permute-done.27.refs_17_
  162.3 10.0 %attention.2 = (bf16[8,64,1024]{2,1,0:T(8,128)(2,1)S(1)}, bf16[4,2,128,256]{3,2,1,0:T(8,128)(2,1)S(1)}) custom-call(s32[130]{0:T(256)S(1)} %tables.1.table, bf16[4,64,2048]{2,1,0:T(8,128)(2,1)S(1)} %bitcast.40, bf16[4,64,2048]{2,1,0:T(8,128)(2,1)S(1)} %bitcast.42, bf16[2,4,64,512]{3,2,1,0:T(8,128)(2,1)S(1)} %bitcast.46, ...), custom_call_target="tpu_custom_call" | custom-call | flops 47244640 | bytes 251658 | tf_op jit(solution)/shard_map/attention/pallas_call | solution.py:355
  172.3 1.3 collective-permute-start.28
  173.6 10.0 %attention.3 = (bf16[8,64,1024]{2,1,0:T(8,128)(2,1)S(1)}, bf16[4,2,128,256]{3,2,1,0:T(8,128)(2,1)S(1)}) custom-call(s32[130]{0:T(256)S(1)} %tables.1.table, bf16[4,64,2048]{2,1,0:T(8,128)(2,1)S(1)} %bitcast.41, bf16[4,64,2048]{2,1,0:T(8,128)(2,1)S(1)} %bitcast.43, bf16[2,4,64,512]{3,2,1,0:T(8,128)(2,1)S(1)} %bitcast.47, ...), custom_call_target="tpu_custom_call" | custom-call | flops 47244640 | bytes 251658 | tf_op jit(solution)/shard_map/attention/pallas_call | solution.py:355
  183.7 2.6 collective-permute-done.28.refs_3_
  186.3 4.8 %send_part.2.refs_3_ = bf16[512,1024]{1,0:T(8,128)(2,1)S(1)} custom-call(s32[130]{0:T(256)S(1)} %tables.1.table, bf16[512,1024]{1,0:T(8,128)(2,1)S(1)} %bitcast.34, bf16[512,1024]{1,0:T(8,128)(2,1)S(1)} %bitcast.37, bf16[2048,5120]{1,0:T(8,128)(2,1)} %refs_2_.9, bf16[4,2,128,256]{3,2,1,0:T(8,128)(2,1)S(1)} %collective-permute-done.28.refs_3_), custom_call_target="tpu_custom_call" | custom-call | flops 42949672 | bytes 146800 | tf_op jit(solution)/shard_map/send_part/pallas_call | solution.py:406
  191.1 1.3 collective-permute-start.29
  192.5 7.2 %send_part.3 = (bf16[512,1024]{1,0:T(8,128)(2,1)S(1)}, bf16[512,512]{1,0:T(8,128)(2,1)}) custom-call(s32[130]{0:T(256)S(1)} %tables.1.table, bf16[512,1024]{1,0:T(8,128)(2,1)S(1)} %bitcast.35, bf16[512,1024]{1,0:T(8,128)(2,1)S(1)} %bitcast.38, bf16[2048,5120]{1,0:T(8,128)(2,1)} %refs_2_.9, bf16[512,1024]{1,0:T(8,128)(2,1)S(1)} %send_part.2.refs_3_), custom_call_target="tpu_custom_call" | custom-call | flops 64424508 | bytes 199229 | tf_op jit(solution)/shard_map/send_part/pallas_call | solution.py:406
  199.6 9.6 %own_part.1 = (bf16[512,1024]{1,0:T(8,128)(2,1)S(1)}, bf16[512,1024]{1,0:T(8,128)(2,1)S(1)}, bf16[512,512]{1,0:T(8,128)(2,1)S(1)}) custom-call(s32[130]{0:T(256)S(1)} %tables.1.table, bf16[512,1024]{1,0:T(8,128)(2,1)S(1)} %bitcast.36, bf16[512,1024]{1,0:T(8,128)(2,1)S(1)} %bitcast.39, bf16[2048,5120]{1,0:T(8,128)(2,1)} %refs_2_.9, ...), custom_call_target="tpu_custom_call" | custom-call | flops 107374184 | bytes 304087 | tf_op jit(solution)/shard_map/own_part/pallas_call | solution.py:406
  212.0 3.6 %collective-permute-done.29 = bf16[512,1024]{1,0:T(8,128)(2,1)S(1)} collective-permute-done((bf16[512,1024]{1,0:T(8,128)(2,1)S(1)}, bf16[512,1024]{1,0:T(8,128)(2,1)S(1)}, u32[]{:S(2)}, u32[]{:S(2)}) %collective-permute-start.29) | collective-permute-done | bytes 1048608 | tf_op jit(solution)/shard_map/ppermute | solution.py:564
  216.8 2.7 residual.3
  219.6 3.8 %collective-permute-start.32 = (bf16[2,64,1024]{2,1,0:T(8,128)(2,1)S(1)}, bf16[2,64,1024]{2,1,0:T(8,128)(2,1)}, u32[]{:S(2)}, u32[]{:S(2)}) collective-permute-start(bf16[2,64,1024]{2,1,0:T(8,128)(2,1)S(1)} %get-tuple-element.72), channel_id=1, source_target_pairs={{0,6},{1,7},{2,0},{3,1},{4,2},{5,3},{6,4},{7,5},{8,14},{9,15},{10,... | collective-permute-start | bytes 786440 | tf_op jit(solution)/shard_map/ppermute | solution.py:524
  223.4 7.3 %collective-permute-done.31.refs_1_ = bf16[2,64,1024]{2,1,0:T(8,128)(2,1)} collective-permute-done((bf16[2,64,1024]{2,1,0:T(8,128)(2,1)S(1)}, bf16[2,64,1024]{2,1,0:T(8,128)(2,1)}, u32[]{:S(2)}, u32[]{:S(2)}) %collective-permute-start.31) | collective-permute-done | bytes 262176 | tf_op jit(solution)/shard_map/ppermute | solution.py:524
  230.8 1.9 collective-permute-done.32.refs_2_
  232.7 10.2 %collective-permute-done.33.refs_3_ = bf16[2,64,1024]{2,1,0:T(8,128)(2,1)} collective-permute-done((bf16[2,64,1024]{2,1,0:T(8,128)(2,1)S(1)}, bf16[2,64,1024]{2,1,0:T(8,128)(2,1)}, u32[]{:S(2)}, u32[]{:S(2)}) %collective-permute-start.33) | collective-permute-done | bytes 262176 | tf_op jit(solution)/shard_map/ppermute | solution.py:524
  244.9 2.7 residual.5
  247.7 3.8 %collective-permute-start.38 = (bf16[2,64,1024]{2,1,0:T(8,128)(2,1)S(1)}, bf16[2,64,1024]{2,1,0:T(8,128)(2,1)S(1)}, u32[]{:S(2)}, u32[]{:S(2)}) collective-permute-start(bf16[2,64,1024]{2,1,0:T(8,128)(2,1)S(1)} %get-tuple-element.80), channel_id=1, source_target_pairs={{0,6},{1,7},{2,0},{3,1},{4,2},{5,3},{6,4},{7,5},{8,14},{9,15},{10,... | collective-permute-start | bytes 786440 | tf_op jit(solution)/shard_map/ppermute | solution.py:524
  251.5 4.6 %collective-permute-done.34 = bf16[512,512]{1,0:T(8,128)(2,1)} collective-permute-done((bf16[512,512]{1,0:T(8,128)(2,1)}, bf16[512,512]{1,0:T(8,128)(2,1)}, u32[]{:S(2)}, u32[]{:S(2)}) %collective-permute-start.34) | collective-permute-done | bytes 524320 | tf_op jit(solution)/shard_map/ppermute | solution.py:564
  256.1 2.0 residual.4
  262.0 3.8 %collective-permute-start.42 = (bf16[2,64,512]{2,1,0:T(8,128)(2,1)S(1)}, bf16[2,64,512]{2,1,0:T(8,128)(2,1)S(1)}, u32[]{:S(2)}, u32[]{:S(2)}) collective-permute-start(bf16[2,64,512]{2,1,0:T(8,128)(2,1)S(1)} %get-tuple-element.84), channel_id=1, source_target_pairs={{0,6},{1,7},{2,0},{3,1},{4,2},{5,3},{6,4},{7,5},{8,14},{9,15},{10,... | collective-permute-start | bytes 393224 | tf_op jit(solution)/shard_map/ppermute | solution.py:524
  266.0 12.0 %collective-permute-done.39.refs_8_ = bf16[2,64,1024]{2,1,0:T(8,128)(2,1)S(1)} collective-permute-done((bf16[2,64,1024]{2,1,0:T(8,128)(2,1)S(1)}, bf16[2,64,1024]{2,1,0:T(8,128)(2,1)S(1)}, u32[]{:S(2)}, u32[]{:S(2)}) %collective-permute-start.39) | collective-permute-done | bytes 262176 | tf_op jit(solution)/shard_map/ppermute | solution.py:524
  278.2 3.2 %collective-permute-done.43.refs_13_ = bf16[2,64,512]{2,1,0:T(8,128)(2,1)S(1)} collective-permute-done((bf16[2,64,512]{2,1,0:T(8,128)(2,1)S(1)}, bf16[2,64,512]{2,1,0:T(8,128)(2,1)S(1)}, u32[]{:S(2)}, u32[]{:S(2)}) %collective-permute-start.43) | collective-permute-done | bytes 131104 | tf_op jit(solution)/shard_map/ppermute | solution.py:524
  282.1 1.6 pad_maximum_fusion
  283.7 3.3 %placed.1 = bf16[512,2560]{1,0:T(8,128)(2,1)} custom-call(s32[130]{0:T(256)S(1)} %tables.1.table, bf16[2,64,1024]{2,1,0:T(8,128)(2,1)S(1)} %get-tuple-element.70.refs_0_, bf16[2,64,1024]{2,1,0:T(8,128)(2,1)} %collective-permute-done.31.refs_1_, bf16[2,64,1024]{2,1,0:T(8,128)(2,1)} %collective-permute-done.32.refs_2_, ...), custom_call_target="tpu_custom_call" | custom-call | bytes 104857 | tf_op jit(solution)/shard_map/placed/pallas_call | solution.py:484
  (132 shorter events, 26.0 us)
Async XLA Ops:
  3.4 40.0 %copy-start.10 = (s32[8]{0:T(128)S(1)}, s32[8]{0:T(128)}, u32[]{:S(2)}) copy-start(s32[8]{0:T(128)} %source.1) | copy-start | bytes 100
  3.4 40.0 %copy-start.11 = (s32[8]{0:T(128)S(1)}, s32[8]{0:T(128)}, u32[]{:S(2)}) copy-start(s32[8]{0:T(128)} %target.1) | copy-start | bytes 100
  3.5 6.3 %collective-permute-start = (bf16[3,64,2560]{2,1,0:T(8,128)(2,1)S(1)}, bf16[3,64,2560]{2,1,0:T(8,128)(2,1)S(1)}, u32[]{:S(2)}, u32[]{:S(2)}) collective-permute-start(bf16[3,64,2560]{2,1,0:T(8,128)(2,1)S(1)} %pad_maximum_fusion.1), channel_id=1, source_target_pairs={{0,1},{1,0},{2,3},{3,2},{4,5},{5,4},{6,7},{7,6},{8,9},{9,8},{10,11... | collective-permute-start | bytes 2949128 | tf_op jit(solution)/shard_map/ppermute | solution.py:524
  4.0 12.7 %collective-permute-start.2 = (bf16[64,2560]{1,0:T(8,128)(2,1)S(1)}, bf16[64,2560]{1,0:T(8,128)(2,1)S(1)}, u32[]{:S(2)}, u32[]{:S(2)}) collective-permute-start(bf16[64,2560]{1,0:T(8,128)(2,1)S(1)} %get-tuple-element.88), channel_id=1, source_target_pairs={{0,3},{1,2},{2,5},{3,4},{4,7},{5,6},{6,1},{7,0},{8,11},{9,10},{10,... | collective-permute-start | bytes 983048 | tf_op jit(solution)/shard_map/ppermute | solution.py:524
  6.7 17.3 %collective-permute-start.1 = (bf16[64,2560]{1,0:T(8,128)(2,1)S(1)}, bf16[64,2560]{1,0:T(8,128)(2,1)S(1)}, u32[]{:S(2)}, u32[]{:S(2)}) collective-permute-start(bf16[64,2560]{1,0:T(8,128)(2,1)S(1)} %get-tuple-element.89), channel_id=1, source_target_pairs={{0,2},{1,3},{2,4},{3,5},{4,6},{5,7},{6,0},{7,1},{8,10},{9,11},{10,... | collective-permute-start | bytes 983048 | tf_op jit(solution)/shard_map/ppermute | solution.py:524
  8.3 15.7 %collective-permute-start.3 = (bf16[64,2560]{1,0:T(8,128)(2,1)S(1)}, bf16[64,2560]{1,0:T(8,128)(2,1)S(1)}, u32[]{:S(2)}, u32[]{:S(2)}) collective-permute-start(bf16[64,2560]{1,0:T(8,128)(2,1)S(1)} %get-tuple-element.93.refs_0_), channel_id=1, source_target_pairs={{0,8},{8,0},{1,9},{9,1},{2,10},{10,2},{3,11},{11,3},{4,12},{12,4},... | collective-permute-start | bytes 983048 | tf_op jit(solution)/shard_map/ppermute | solution.py:564
  9.8 53.8 %copy-start.7 = (bf16[128]{0:T(256)(128)(2,1)S(1)}, bf16[128]{0:T(256)(128)(2,1)}, u32[]{:S(2)}) copy-start(bf16[128]{0:T(256)(128)(2,1)} %param.18) | copy-start | bytes 772
  9.8 14.2 %collective-permute-start.7 = (bf16[1,2560]{1,0:T(2,128)(2,1)S(1)}, bf16[1,2560]{1,0:T(2,128)(2,1)S(1)}, u32[]{:S(2)}, u32[]{:S(2)}) collective-permute-start(bf16[1,2560]{1,0:T(2,128)(2,1)S(1)} %broadcast_in_dim.6.refs_8_.refs_6_), channel_id=1, source_target_pairs={{0,8},{8,0},{1,9},{9,1},{2,10},{10,2},{3,11},{11,3},{4,12},{12,4},... | collective-permute-start | bytes 15368 | tf_op jit(solution)/shard_map/ppermute | solution.py:564
  11.2 13.7 %collective-permute-start.4 = (bf16[64,2560]{1,0:T(8,128)(2,1)S(1)}, bf16[64,2560]{1,0:T(8,128)(2,1)S(1)}, u32[]{:S(2)}, u32[]{:S(2)}) collective-permute-start(bf16[64,2560]{1,0:T(8,128)(2,1)S(1)} %get-tuple-element.100.refs_1_), channel_id=1, source_target_pairs={{0,8},{8,0},{1,9},{9,1},{2,10},{10,2},{3,11},{11,3},{4,12},{12,4},... | collective-permute-start | bytes 983048 | tf_op jit(solution)/shard_map/ppermute | solution.py:564
  25.6 16.3 %collective-permute-start.8 = (bf16[128,2560]{1,0:T(8,128)(2,1)S(1)}, bf16[128,2560]{1,0:T(8,128)(2,1)S(1)}, u32[]{:S(2)}, u32[]{:S(2)}) collective-permute-start(bf16[128,2560]{1,0:T(8,128)(2,1)S(1)} %pad_maximum_fusion.2), channel_id=1, source_target_pairs={{0,6},{1,7},{2,0},{3,1},{4,2},{5,3},{6,4},{7,5},{8,14},{9,15},{10,... | collective-permute-start | bytes 1966088 | tf_op jit(solution)/shard_map/ppermute | solution.py:524
  27.9 17.0 %collective-permute-start.6 = (bf16[64,2560]{1,0:T(8,128)(2,1)S(1)}, bf16[64,2560]{1,0:T(8,128)(2,1)S(1)}, u32[]{:S(2)}, u32[]{:S(2)}) collective-permute-start(bf16[64,2560]{1,0:T(8,128)(2,1)S(1)} %collective-permute-done.2.refs_3_), channel_id=1, source_target_pairs={{0,8},{8,0},{1,9},{9,1},{2,10},{10,2},{3,11},{11,3},{4,12},{12,4},... | collective-permute-start | bytes 983048 | tf_op jit(solution)/shard_map/ppermute | solution.py:564
  29.4 15.5 %collective-permute-start.5 = (bf16[64,2560]{1,0:T(8,128)(2,1)S(1)}, bf16[64,2560]{1,0:T(8,128)(2,1)S(1)}, u32[]{:S(2)}, u32[]{:S(2)}) collective-permute-start(bf16[64,2560]{1,0:T(8,128)(2,1)S(1)} %collective-permute-done.1.refs_2_), channel_id=1, source_target_pairs={{0,8},{8,0},{1,9},{9,1},{2,10},{10,2},{3,11},{11,3},{4,12},{12,4},... | collective-permute-start | bytes 983048 | tf_op jit(solution)/shard_map/ppermute | solution.py:564
  42.0 20.4 %collective-permute-start.10 = (bf16[128,2560]{1,0:T(8,128)(2,1)S(1)}, bf16[128,2560]{1,0:T(8,128)(2,1)S(1)}, u32[]{:S(2)}, u32[]{:S(2)}) collective-permute-start(bf16[128,2560]{1,0:T(8,128)(2,1)S(1)} %collective-permute-done.8.refs_0_.refs_4_), channel_id=1, source_target_pairs={{0,8},{8,0},{1,9},{9,1},{2,10},{10,2},{3,11},{11,3},{4,12},{12,4},... | collective-permute-start | bytes 1966088 | tf_op jit(solution)/shard_map/ppermute | solution.py:564
  46.3 16.0 %collective-permute-start.9 = (bf16[64,2560]{1,0:T(8,128)(2,1)}, bf16[64,2560]{1,0:T(8,128)(2,1)S(1)}, u32[]{:S(2)}, u32[]{:S(2)}) collective-permute-start(bf16[64,2560]{1,0:T(8,128)(2,1)} %get-tuple-element.48), channel_id=1, source_target_pairs={{0,4},{1,5},{2,6},{3,7},{4,0},{5,1},{6,2},{7,3},{8,12},{9,13},{10,... | collective-permute-start | bytes 983048 | tf_op jit(solution)/shard_map/ppermute | solution.py:524
  62.4 16.5 %collective-permute-start.11 = (bf16[64,2560]{1,0:T(8,128)(2,1)}, bf16[64,2560]{1,0:T(8,128)(2,1)S(1)}, u32[]{:S(2)}, u32[]{:S(2)}) collective-permute-start(bf16[64,2560]{1,0:T(8,128)(2,1)} %get-tuple-element.49), channel_id=1, source_target_pairs={{0,4},{1,5},{2,6},{3,7},{4,0},{5,1},{6,2},{7,3},{8,12},{9,13},{10,... | collective-permute-start | bytes 983048 | tf_op jit(solution)/shard_map/ppermute | solution.py:524
  72.3 9.7 %collective-permute-start.12 = (bf16[64,2560]{1,0:T(8,128)(2,1)S(1)}, bf16[64,2560]{1,0:T(8,128)(2,1)S(1)}, u32[]{:S(2)}, u32[]{:S(2)}) collective-permute-start(bf16[64,2560]{1,0:T(8,128)(2,1)S(1)} %collective-permute-done.9.refs_1_.refs_5_), channel_id=1, source_target_pairs={{0,8},{8,0},{1,9},{9,1},{2,10},{10,2},{3,11},{11,3},{4,12},{12,4},... | collective-permute-start | bytes 983048 | tf_op jit(solution)/shard_map/ppermute | solution.py:564
  78.9 9.9 %collective-permute-start.13 = (bf16[64,2560]{1,0:T(8,128)(2,1)S(1)}, bf16[64,2560]{1,0:T(8,128)(2,1)S(1)}, u32[]{:S(2)}, u32[]{:S(2)}) collective-permute-start(bf16[64,2560]{1,0:T(8,128)(2,1)S(1)} %collective-permute-done.11.refs_2_.refs_6_), channel_id=1, source_target_pairs={{0,8},{8,0},{1,9},{9,1},{2,10},{10,2},{3,11},{11,3},{4,12},{12,4},... | collective-permute-start | bytes 983048 | tf_op jit(solution)/shard_map/ppermute | solution.py:564
  79.8 20.4 %collective-permute-start.16 = (bf16[2,4,64,512]{3,2,1,0:T(8,128)(2,1)S(1)}, bf16[2,4,64,512]{3,2,1,0:T(8,128)(2,1)S(1)}, u32[]{:S(2)}, u32[]{:S(2)}) collective-permute-start(bf16[2,4,64,512]{3,2,1,0:T(8,128)(2,1)S(1)} %bitcast.44), channel_id=1, source_target_pairs={{0,2},{1,3},{2,4},{3,5},{4,6},{5,7},{6,0},{7,1},{8,10},{9,11},{10,... | collective-permute-start | bytes 1572872 | tf_op jit(solution)/shard_map/ppermute | solution.py:524
  98.2 25.9 %collective-permute-start.17 = (bf16[2,4,64,512]{3,2,1,0:T(8,128)(2,1)S(1)}, bf16[2,4,64,512]{3,2,1,0:T(8,128)(2,1)S(1)}, u32[]{:S(2)}, u32[]{:S(2)}) collective-permute-start(bf16[2,4,64,512]{3,2,1,0:T(8,128)(2,1)S(1)} %bitcast.48), channel_id=1, source_target_pairs={{0,2},{1,3},{2,4},{3,5},{4,6},{5,7},{6,0},{7,1},{8,10},{9,11},{10,... | collective-permute-start | bytes 1572872 | tf_op jit(solution)/shard_map/ppermute | solution.py:524
  100.2 24.6 %collective-permute-start.20 = (bf16[2,4,64,512]{3,2,1,0:T(8,128)(2,1)S(1)}, bf16[2,4,64,512]{3,2,1,0:T(8,128)(2,1)S(1)}, u32[]{:S(2)}, u32[]{:S(2)}) collective-permute-start(bf16[2,4,64,512]{3,2,1,0:T(8,128)(2,1)S(1)} %collective-permute-done.16.refs_6_), channel_id=1, source_target_pairs={{0,2},{1,3},{2,4},{3,5},{4,6},{5,7},{6,0},{7,1},{8,10},{9,11},{10,... | collective-permute-start | bytes 1572872 | tf_op jit(solution)/shard_map/ppermute | solution.py:524
  124.2 16.7 %collective-permute-start.21 = (bf16[2,4,64,512]{3,2,1,0:T(8,128)(2,1)S(1)}, bf16[2,4,64,512]{3,2,1,0:T(8,128)(2,1)S(1)}, u32[]{:S(2)}, u32[]{:S(2)}) collective-permute-start(bf16[2,4,64,512]{3,2,1,0:T(8,128)(2,1)S(1)} %collective-permute-done.17.refs_7_), channel_id=1, source_target_pairs={{0,2},{1,3},{2,4},{3,5},{4,6},{5,7},{6,0},{7,1},{8,10},{9,11},{10,... | collective-permute-start | bytes 1572872 | tf_op jit(solution)/shard_map/ppermute | solution.py:524
  124.3 16.6 %collective-permute-start.14 = (bf16[2,4,64,512]{3,2,1,0:T(8,128)(2,1)S(1)}, bf16[2,4,64,512]{3,2,1,0:T(8,128)(2,1)S(1)}, u32[]{:S(2)}, u32[]{:S(2)}) collective-permute-start(bf16[2,4,64,512]{3,2,1,0:T(8,128)(2,1)S(1)} %bitcast.45), channel_id=1, source_target_pairs={{0,1},{1,0},{2,3},{3,2},{4,5},{5,4},{6,7},{7,6},{8,9},{9,8},{10,11... | collective-permute-start | bytes 1572872 | tf_op jit(solution)/shard_map/ppermute | solution.py:524
  124.3 16.6 %collective-permute-start.18 = (bf16[2,4,64,512]{3,2,1,0:T(8,128)(2,1)S(1)}, bf16[2,4,64,512]{3,2,1,0:T(8,128)(2,1)S(1)}, u32[]{:S(2)}, u32[]{:S(2)}) collective-permute-start(bf16[2,4,64,512]{3,2,1,0:T(8,128)(2,1)S(1)} %collective-permute-done.16.refs_6_), channel_id=1, source_target_pairs={{0,1},{1,0},{2,3},{3,2},{4,5},{5,4},{6,7},{7,6},{8,9},{9,8},{10,11... | collective-permute-start | bytes 1572872 | tf_op jit(solution)/shard_map/ppermute | solution.py:524
  124.8 27.3 %collective-permute-start.22 = (bf16[2,4,64,512]{3,2,1,0:T(8,128)(2,1)S(1)}, bf16[2,4,64,512]{3,2,1,0:T(8,128)(2,1)S(1)}, u32[]{:S(2)}, u32[]{:S(2)}) collective-permute-start(bf16[2,4,64,512]{3,2,1,0:T(8,128)(2,1)S(1)} %collective-permute-done.20.refs_10_), channel_id=1, source_target_pairs={{0,1},{1,0},{2,3},{3,2},{4,5},{5,4},{6,7},{7,6},{8,9},{9,8},{10,11... | collective-permute-start | bytes 1572872 | tf_op jit(solution)/shard_map/ppermute | solution.py:524
  124.9 27.2 %collective-permute-start.24 = (bf16[2,4,64,512]{3,2,1,0:T(8,128)(2,1)S(1)}, bf16[2,4,64,512]{3,2,1,0:T(8,128)(2,1)S(1)}, u32[]{:S(2)}, u32[]{:S(2)}) collective-permute-start(bf16[2,4,64,512]{3,2,1,0:T(8,128)(2,1)S(1)} %collective-permute-done.20.refs_10_), channel_id=1, source_target_pairs={{0,2},{1,3},{2,4},{3,5},{4,6},{5,7},{6,0},{7,1},{8,10},{9,11},{10,... | collective-permute-start | bytes 1572872 | tf_op jit(solution)/shard_map/ppermute | solution.py:524
  140.9 19.4 %collective-permute-start.25 = (bf16[2,4,64,512]{3,2,1,0:T(8,128)(2,1)S(1)}, bf16[2,4,64,512]{3,2,1,0:T(8,128)(2,1)S(1)}, u32[]{:S(2)}, u32[]{:S(2)}) collective-permute-start(bf16[2,4,64,512]{3,2,1,0:T(8,128)(2,1)S(1)} %collective-permute-done.21.refs_11_), channel_id=1, source_target_pairs={{0,2},{1,3},{2,4},{3,5},{4,6},{5,7},{6,0},{7,1},{8,10},{9,11},{10,... | collective-permute-start | bytes 1572872 | tf_op jit(solution)/shard_map/ppermute | solution.py:524
  140.9 19.4 %collective-permute-start.15 = (bf16[2,4,64,512]{3,2,1,0:T(8,128)(2,1)S(1)}, bf16[2,4,64,512]{3,2,1,0:T(8,128)(2,1)S(1)}, u32[]{:S(2)}, u32[]{:S(2)}) collective-permute-start(bf16[2,4,64,512]{3,2,1,0:T(8,128)(2,1)S(1)} %bitcast.49), channel_id=1, source_target_pairs={{0,1},{1,0},{2,3},{3,2},{4,5},{5,4},{6,7},{7,6},{8,9},{9,8},{10,11... | collective-permute-start | bytes 1572872 | tf_op jit(solution)/shard_map/ppermute | solution.py:524
  140.9 19.4 %collective-permute-start.19 = (bf16[2,4,64,512]{3,2,1,0:T(8,128)(2,1)S(1)}, bf16[2,4,64,512]{3,2,1,0:T(8,128)(2,1)S(1)}, u32[]{:S(2)}, u32[]{:S(2)}) collective-permute-start(bf16[2,4,64,512]{3,2,1,0:T(8,128)(2,1)S(1)} %collective-permute-done.17.refs_7_), channel_id=1, source_target_pairs={{0,1},{1,0},{2,3},{3,2},{4,5},{5,4},{6,7},{7,6},{8,9},{9,8},{10,11... | collective-permute-start | bytes 1572872 | tf_op jit(solution)/shard_map/ppermute | solution.py:524
  152.1 8.2 %collective-permute-start.26 = (bf16[2,4,64,512]{3,2,1,0:T(8,128)(2,1)S(1)}, bf16[2,4,64,512]{3,2,1,0:T(8,128)(2,1)S(1)}, u32[]{:S(2)}, u32[]{:S(2)}) collective-permute-start(bf16[2,4,64,512]{3,2,1,0:T(8,128)(2,1)S(1)} %collective-permute-done.24.refs_14_), channel_id=1, source_target_pairs={{0,1},{1,0},{2,3},{3,2},{4,5},{5,4},{6,7},{7,6},{8,9},{9,8},{10,11... | collective-permute-start | bytes 1572872 | tf_op jit(solution)/shard_map/ppermute | solution.py:524
  152.1 8.2 %collective-permute-start.23 = (bf16[2,4,64,512]{3,2,1,0:T(8,128)(2,1)S(1)}, bf16[2,4,64,512]{3,2,1,0:T(8,128)(2,1)S(1)}, u32[]{:S(2)}, u32[]{:S(2)}) collective-permute-start(bf16[2,4,64,512]{3,2,1,0:T(8,128)(2,1)S(1)} %collective-permute-done.21.refs_11_), channel_id=1, source_target_pairs={{0,1},{1,0},{2,3},{3,2},{4,5},{5,4},{6,7},{7,6},{8,9},{9,8},{10,11... | collective-permute-start | bytes 1572872 | tf_op jit(solution)/shard_map/ppermute | solution.py:524
  160.3 1.9 collective-permute-start.27
  172.3 14.0 %collective-permute-start.28 = (bf16[4,2,128,256]{3,2,1,0:T(8,128)(2,1)S(1)}, bf16[4,2,128,256]{3,2,1,0:T(8,128)(2,1)S(1)}, u32[]{:S(2)}, u32[]{:S(2)}) collective-permute-start(bf16[4,2,128,256]{3,2,1,0:T(8,128)(2,1)S(1)} %get-tuple-element.60), channel_id=1, source_target_pairs={{0,8},{8,0},{1,9},{9,1},{2,10},{10,2},{3,11},{11,3},{4,12},{12,4},... | collective-permute-start | bytes 1572872 | tf_op jit(solution)/shard_map/ppermute | solution.py:564
  191.1 24.4 %collective-permute-start.29 = (bf16[512,1024]{1,0:T(8,128)(2,1)S(1)}, bf16[512,1024]{1,0:T(8,128)(2,1)S(1)}, u32[]{:S(2)}, u32[]{:S(2)}) collective-permute-start(bf16[512,1024]{1,0:T(8,128)(2,1)S(1)} %send_part.2.refs_3_), channel_id=1, source_target_pairs={{0,8},{8,0},{1,9},{9,1},{2,10},{10,2},{3,11},{11,3},{4,12},{12,4},... | collective-permute-start | bytes 3145736 | tf_op jit(solution)/shard_map/ppermute | solution.py:564
  215.6 27.3 %collective-permute-start.30 = (bf16[512,1024]{1,0:T(8,128)(2,1)S(1)}, bf16[512,1024]{1,0:T(8,128)(2,1)S(1)}, u32[]{:S(2)}, u32[]{:S(2)}) collective-permute-start(bf16[512,1024]{1,0:T(8,128)(2,1)S(1)} %get-tuple-element.69), channel_id=1, source_target_pairs={{0,8},{8,0},{1,9},{9,1},{2,10},{10,2},{3,11},{11,3},{4,12},{12,4},... | collective-permute-start | bytes 3145736 | tf_op jit(solution)/shard_map/ppermute | solution.py:564
  219.6 11.2 %collective-permute-start.31 = (bf16[2,64,1024]{2,1,0:T(8,128)(2,1)S(1)}, bf16[2,64,1024]{2,1,0:T(8,128)(2,1)}, u32[]{:S(2)}, u32[]{:S(2)}) collective-permute-start(bf16[2,64,1024]{2,1,0:T(8,128)(2,1)S(1)} %get-tuple-element.71), channel_id=1, source_target_pairs={{0,2},{1,3},{2,4},{3,5},{4,6},{5,7},{6,0},{7,1},{8,10},{9,11},{10,... | collective-permute-start | bytes 786440 | tf_op jit(solution)/shard_map/ppermute | solution.py:524
  219.6 13.1 %collective-permute-start.32 = (bf16[2,64,1024]{2,1,0:T(8,128)(2,1)S(1)}, bf16[2,64,1024]{2,1,0:T(8,128)(2,1)}, u32[]{:S(2)}, u32[]{:S(2)}) collective-permute-start(bf16[2,64,1024]{2,1,0:T(8,128)(2,1)S(1)} %get-tuple-element.72), channel_id=1, source_target_pairs={{0,6},{1,7},{2,0},{3,1},{4,2},{5,3},{6,4},{7,5},{8,14},{9,15},{10,... | collective-permute-start | bytes 786440 | tf_op jit(solution)/shard_map/ppermute | solution.py:524
  223.4 19.4 %collective-permute-start.33 = (bf16[2,64,1024]{2,1,0:T(8,128)(2,1)S(1)}, bf16[2,64,1024]{2,1,0:T(8,128)(2,1)}, u32[]{:S(2)}, u32[]{:S(2)}) collective-permute-start(bf16[2,64,1024]{2,1,0:T(8,128)(2,1)S(1)} %get-tuple-element.73), channel_id=1, source_target_pairs={{0,4},{1,5},{2,6},{3,7},{4,0},{5,1},{6,2},{7,3},{8,12},{9,13},{10,... | collective-permute-start | bytes 786440 | tf_op jit(solution)/shard_map/ppermute | solution.py:524
  243.8 12.3 %collective-permute-start.34 = (bf16[512,512]{1,0:T(8,128)(2,1)}, bf16[512,512]{1,0:T(8,128)(2,1)}, u32[]{:S(2)}, u32[]{:S(2)}) collective-permute-start(bf16[512,512]{1,0:T(8,128)(2,1)} %get-tuple-element.74.refs_3_), channel_id=1, source_target_pairs={{0,8},{8,0},{1,9},{9,1},{2,10},{10,2},{3,11},{11,3},{4,12},{12,4},... | collective-permute-start | bytes 1572872 | tf_op jit(solution)/shard_map/ppermute | solution.py:564
  247.6 14.4 %collective-permute-start.37 = (bf16[2,64,1024]{2,1,0:T(8,128)(2,1)S(1)}, bf16[2,64,1024]{2,1,0:T(8,128)(2,1)S(1)}, u32[]{:S(2)}, u32[]{:S(2)}) collective-permute-start(bf16[2,64,1024]{2,1,0:T(8,128)(2,1)S(1)} %get-tuple-element.79), channel_id=1, source_target_pairs={{0,2},{1,3},{2,4},{3,5},{4,6},{5,7},{6,0},{7,1},{8,10},{9,11},{10,... | collective-permute-start | bytes 786440 | tf_op jit(solution)/shard_map/ppermute | solution.py:524
  247.7 18.1 %collective-permute-start.38 = (bf16[2,64,1024]{2,1,0:T(8,128)(2,1)S(1)}, bf16[2,64,1024]{2,1,0:T(8,128)(2,1)S(1)}, u32[]{:S(2)}, u32[]{:S(2)}) collective-permute-start(bf16[2,64,1024]{2,1,0:T(8,128)(2,1)S(1)} %get-tuple-element.80), channel_id=1, source_target_pairs={{0,6},{1,7},{2,0},{3,1},{4,2},{5,3},{6,4},{7,5},{8,14},{9,15},{10,... | collective-permute-start | bytes 786440 | tf_op jit(solution)/shard_map/ppermute | solution.py:524
  251.5 26.5 %collective-permute-start.39 = (bf16[2,64,1024]{2,1,0:T(8,128)(2,1)S(1)}, bf16[2,64,1024]{2,1,0:T(8,128)(2,1)S(1)}, u32[]{:S(2)}, u32[]{:S(2)}) collective-permute-start(bf16[2,64,1024]{2,1,0:T(8,128)(2,1)S(1)} %get-tuple-element.81), channel_id=1, source_target_pairs={{0,4},{1,5},{2,6},{3,7},{4,0},{5,1},{6,2},{7,3},{8,12},{9,13},{10,... | collective-permute-start | bytes 786440 | tf_op jit(solution)/shard_map/ppermute | solution.py:524
  258.1 23.2 %collective-permute-start.35 = (bf16[4,2,128,256]{3,2,1,0:T(8,128)(2,1)S(1)}, bf16[4,2,128,256]{3,2,1,0:T(8,128)(2,1)S(1)}, u32[]{:S(2)}, u32[]{:S(2)}) collective-permute-start(bf16[4,2,128,256]{3,2,1,0:T(8,128)(2,1)S(1)} %copy-done.3), channel_id=1, source_target_pairs={{0,8},{8,0},{1,9},{9,1},{2,10},{10,2},{3,11},{11,3},{4,12},{12,4},... | collective-permute-start | bytes 1572872 | tf_op jit(solution)/shard_map/ppermute | solution.py:564
  262.0 16.2 %collective-permute-start.41 = (bf16[2,64,512]{2,1,0:T(8,128)(2,1)S(1)}, bf16[2,64,512]{2,1,0:T(8,128)(2,1)S(1)}, u32[]{:S(2)}, u32[]{:S(2)}) collective-permute-start(bf16[2,64,512]{2,1,0:T(8,128)(2,1)S(1)} %get-tuple-element.83), channel_id=1, source_target_pairs={{0,2},{1,3},{2,4},{3,5},{4,6},{5,7},{6,0},{7,1},{8,10},{9,11},{10,... | collective-permute-start | bytes 393224 | tf_op jit(solution)/shard_map/ppermute | solution.py:524
  262.0 16.1 %collective-permute-start.42 = (bf16[2,64,512]{2,1,0:T(8,128)(2,1)S(1)}, bf16[2,64,512]{2,1,0:T(8,128)(2,1)S(1)}, u32[]{:S(2)}, u32[]{:S(2)}) collective-permute-start(bf16[2,64,512]{2,1,0:T(8,128)(2,1)S(1)} %get-tuple-element.84), channel_id=1, source_target_pairs={{0,6},{1,7},{2,0},{3,1},{4,2},{5,3},{6,4},{7,5},{8,14},{9,15},{10,... | collective-permute-start | bytes 393224 | tf_op jit(solution)/shard_map/ppermute | solution.py:524
  265.8 15.5 %collective-permute-start.43 = (bf16[2,64,512]{2,1,0:T(8,128)(2,1)S(1)}, bf16[2,64,512]{2,1,0:T(8,128)(2,1)S(1)}, u32[]{:S(2)}, u32[]{:S(2)}) collective-permute-start(bf16[2,64,512]{2,1,0:T(8,128)(2,1)S(1)} %get-tuple-element.85), channel_id=1, source_target_pairs={{0,4},{1,5},{2,6},{3,7},{4,0},{5,1},{6,2},{7,3},{8,12},{9,13},{10,... | collective-permute-start | bytes 393224 | tf_op jit(solution)/shard_map/ppermute | solution.py:524
  278.0 5.7 %collective-permute-start.36 = (bf16[4,64,1024]{2,1,0:T(8,128)(2,1)S(1)}, bf16[4,64,1024]{2,1,0:T(8,128)(2,1)S(1)}, u32[]{:S(2)}, u32[]{:S(2)}) collective-permute-start(bf16[4,64,1024]{2,1,0:T(8,128)(2,1)S(1)} %pad_maximum_fusion.3), channel_id=1, source_target_pairs={{0,1},{1,0},{2,3},{3,2},{4,5},{5,4},{6,7},{7,6},{8,9},{9,8},{10,11... | collective-permute-start | bytes 1572872 | tf_op jit(solution)/shard_map/ppermute | solution.py:524
  281.4 2.4 collective-permute-start.40
  281.5 2.2 collective-permute-start.44
  (20 other events, 178.1 us)
